TPU v7x, 256 devices: a whole 4x4x8 slice. The times are simulated.
256 devices in a mesh: pulse: 32 (over z, x), band: 8 (over y, core).
Axes of the slice: x: 4, y: 4, z: 8, core: 2. Of those that a mesh axis runs over, the one named last changes fastest.
Arguments:
- echoes: bfloat16 [2, 512, 32768], P(None, 'pulse', 'band'), may hold values from -6 to 6
- replica: bfloat16 [2, 2048], replicated, may hold values from -0.125 to 0.125
- pulse_angles: float32 [3, 512], replicated, may hold values from -3.140625 to 3.140625
- footprint: int32 [32, 8], replicated, may hold values from -1 to 127, as said below
- tile_slot: int32 [128], replicated, may hold values from 0 to 127, as said below
- offsets: int32 [512, 8], replicated, may hold values from 0 to 3840
Outputs:
- image_tiles: float32 [2, 128, 2048, 256], P(None, 'pulse', 'band')
- phase_gradient: float32 [512], P('pulse')
Inputs may be any that keep to these rules, and one draw needn't show every extreme that they name: `footprint`: row d lists distinct tiles touched by pulse block d, live entries first and -1 after them; each row has 4 to 8 live entries and some row is full. Live entries whose tiles have the same owner (tile_slot // 4) stand next to each other in groups of 1, only the last group of a row may be shorter; some owner has 1 tiles in every row. A permutation: tile t has slot tile_slot[t], its owner is index tile_slot[t] // 4 of the pulse axis.
All inputs are finite; a program needn't handle non-finite values.
Results may differ from a plain program's by a relative error of at most 0.017.
Values may be sent and summed in bfloat16 or wider, within the bound.
No kernel may reach another device: no remote copies, remote signals or barrier semaphores. Data moves between devices by JAX's collectives and lax.ppermute only.
A program may use at most 384 MiB of HBM per device.

v0:
```python
import math

import jax
import jax.numpy as jnp
from jax import lax
from jax.sharding import PartitionSpec as P

TILE = 256
TAPS = 2048
RB = 4096
P_DEV = 16
FOOT = 8
TILES_DEV = 4


def passed_along(shard, axis, by):
    length = lax.axis_size(axis)
    pairs = [(i, i + by) for i in range(length) if 0 <= i + by < length]
    return lax.ppermute(shard, axis, pairs)


def toeplitz_taps(replica):
    filler = jnp.zeros((2, TILE + 1), replica.dtype)
    padded = jnp.concatenate([replica, filler], axis=1)
    length = padded.shape[1]
    repeated = jnp.tile(padded, (1, TILE))[:, : TILE * (length - 1)]
    shifted = jnp.transpose(repeated.reshape(2, TILE, length - 1), (0, 2, 1))
    real_tap = shifted[0]
    imag_tap = shifted[1]
    first_out = jnp.stack([real_tap, imag_tap])
    second_out = jnp.stack([-imag_tap, real_tap])
    return jnp.stack([first_out, second_out], axis=2)


def compress(echoes, replica, range_tail):
    extended = jnp.concatenate([echoes, range_tail], axis=2)
    pulse_count = echoes.shape[1]
    block_count = RB // TILE
    span_count = TAPS // TILE + 1
    pieces = extended.reshape(2, pulse_count, block_count + span_count - 1, TILE)
    window = jnp.concatenate(
        [pieces[:, :, shift_idx : shift_idx + block_count] for shift_idx in range(span_count)],
        axis=3,
    )
    matrix = toeplitz_taps(replica)
    result = jnp.einsum("cpnu,cudm->dpnm", window, matrix, preferred_element_type=jnp.float32)
    return result.reshape(2, pulse_count, RB).astype(jnp.bfloat16)


def steer_table(omega):
    column = jnp.arange(TILE, dtype=jnp.float32)
    phases = omega[:, None] * column[None, :]
    cosine = jnp.cos(phases).astype(jnp.bfloat16)
    sine_part = jnp.sin(phases).astype(jnp.bfloat16)
    upper_half = jnp.stack([cosine, sine_part], axis=1)
    lower_half = jnp.stack([-sine_part, cosine], axis=1)
    return jnp.stack([upper_half, lower_half])


def pick_rows(packed, starts):

    def per_pulse(series, firsts):

        def per_slot(first_index):
            return lax.dynamic_slice_in_dim(series, first_index, TILE, 1)

        return jax.vmap(per_slot)(firsts)

    picked = jax.vmap(per_pulse, in_axes=(1, 0))(packed, starts)
    return jnp.transpose(picked, (1, 2, 0, 3))


def rotated(picked, kappa, phase, tile_ids, factor):
    rotation = kappa[None, :] * tile_ids.astype(jnp.float32)[:, None] + phase[None, :]
    cosine = jnp.cos(rotation)[:, :, None]
    sine_part = jnp.sin(rotation)[:, :, None]
    real_part = picked[:, 0].astype(jnp.float32)
    imag_part = picked[:, 1].astype(jnp.float32)
    rot_real = (real_part * cosine - imag_part * sine_part) * factor
    rot_imag = (real_part * sine_part + imag_part * cosine) * factor
    return jnp.stack([rot_real, rot_imag], axis=1).astype(jnp.bfloat16)


def sharp_weight(image_sum, comp_axis):
    real_part = jnp.take(image_sum, 0, axis=comp_axis)
    imag_part = jnp.take(image_sum, 1, axis=comp_axis)
    power = real_part * real_part + imag_part * imag_part
    return jnp.stack([power * real_part, -power * imag_part], axis=comp_axis).astype(jnp.bfloat16)


def gradient_terms(picked_rows, weight, steering):
    projected = jnp.einsum("kcij,cqdj->kdqi", weight, steering, preferred_element_type=jnp.float32)
    rows_wide = picked_rows.astype(jnp.float32)
    terms = rows_wide[:, 0] * projected[:, 1] + rows_wide[:, 1] * projected[:, 0]
    return -4.0 * jnp.sum(terms, axis=(0, 2))


def slot_ranks(owner_row, live_row):
    slot_order = jnp.arange(owner_row.shape[0])
    earlier = (
        (owner_row[:, None] == owner_row[None, :])
        & live_row[None, :]
        & (slot_order[None, :] < slot_order[:, None])
    )
    return jnp.sum(earlier, axis=1)


def on_device(echoes, replica, pulse_angles, footprint, tile_slot, offsets):
    node_count = lax.axis_size("pulse")
    my_index = lax.axis_index("pulse")
    slot_cap = max(1, 2 * FOOT // node_count)
    factor = 0.5 / math.sqrt(P_DEV)
    range_tail = passed_along(echoes[:, :, :TAPS], "band", -1)
    packed = compress(echoes, replica, range_tail)
    angle_rows = lax.dynamic_slice_in_dim(pulse_angles, my_index * P_DEV, P_DEV, 1)
    my_offsets = lax.dynamic_slice_in_dim(offsets, my_index * P_DEV, P_DEV, 0)
    steering = steer_table(angle_rows[0])
    owner_of = tile_slot // TILES_DEV
    all_live = footprint >= 0
    all_safe = jnp.maximum(footprint, 0)
    all_owner = owner_of[all_safe]
    all_rank = jax.vmap(slot_ranks)(all_owner, all_live)
    my_live = lax.dynamic_index_in_dim(all_live, my_index, 0, keepdims=False)
    my_tiles = lax.dynamic_index_in_dim(all_safe, my_index, 0, keepdims=False)
    my_owner = lax.dynamic_index_in_dim(all_owner, my_index, 0, keepdims=False)
    my_rank = lax.dynamic_index_in_dim(all_rank, my_index, 0, keepdims=False)
    picked_rows = rotated(
        pick_rows(packed, my_offsets), angle_rows[1], angle_rows[2], my_tiles, factor
    )
    slot_total = node_count * slot_cap
    destination = my_owner * slot_cap + my_rank
    send_map = (
        (destination[None, :] == jnp.arange(slot_total)[:, None]) & my_live[None, :]
    ).astype(jnp.bfloat16)
    source_slot = jnp.arange(node_count)[:, None] * slot_cap + all_rank
    local_ids = tile_slot[all_safe] % TILES_DEV
    chosen = (all_live & (all_owner == my_index)).astype(jnp.float32)
    by_local = (local_ids[:, :, None] == jnp.arange(TILES_DEV)[None, None, :]).astype(
        jnp.float32
    ) * chosen[:, :, None]
    by_slot = (source_slot[:, :, None] == jnp.arange(slot_total)[None, None, :]).astype(jnp.float32)
    recv_map = jnp.einsum("skl,skm->lm", by_local, by_slot).astype(jnp.bfloat16)
    partial_value = jnp.einsum(
        "kcqi,cqdj->kdij", picked_rows, steering, preferred_element_type=jnp.float32
    )
    partial_value = jnp.where(my_live[:, None, None, None], partial_value, jnp.float32(0.0)).astype(
        jnp.bfloat16
    )
    outgoing = jnp.einsum(
        "mk,kdij->mdij", send_map, partial_value, preferred_element_type=jnp.bfloat16
    )
    image_part = jnp.einsum(
        "lm,mdij->dlij",
        recv_map,
        lax.all_to_all(outgoing, "pulse", split_axis=0, concat_axis=0, tiled=True),
        preferred_element_type=jnp.float32,
    )
    weight = sharp_weight(image_part, 0)
    returned = jnp.einsum("lm,dlij->mdij", recv_map, weight, preferred_element_type=jnp.bfloat16)
    arrived = lax.all_to_all(returned, "pulse", split_axis=0, concat_axis=0, tiled=True)
    image_own, arrived = (image_part, arrived)
    slot_weight = jnp.einsum(
        "mk,mdij->kdij", send_map, arrived, preferred_element_type=jnp.bfloat16
    )
    local_grad = gradient_terms(picked_rows, slot_weight, steering)
    band_grad = lax.psum(local_grad, "band")
    square_sum = lax.psum(jnp.sum(band_grad * band_grad), "pulse")
    phase_gradient = band_grad / jnp.sqrt(square_sum / (P_DEV * node_count) + 1e-05)
    return (image_own, phase_gradient)


def solution(mesh):
    placed = (P(None, "pulse", "band"), P(), P(), P(), P(), P())
    return jax.shard_map(
        on_device,
        mesh=mesh,
        in_specs=placed,
        out_specs=(P(None, "pulse", "band", None), P("pulse")),
        check_vma=False,
    )
```

profile of v0, /device:TPU:128, one launch (start us, length us, event | category | flops | bytes accessed | tf_op | source)
XLA Modules:
  0.0 663.2 jit_solution(16949015521423302193)
XLA Ops:
  0.6 1.6 slice.71
  2.2 1.3 collective-permute-start
  7.2 1.9 gather_fusion
  10.5 5.1 reshape.360
  15.6 4.9 tile.10
  20.6 1.7 slice.124
  22.3 1.6 copy.161
  23.9 2.8 copy.97
  26.8 1.2 slice_negate_fusion
  28.7 1.2 fusion.66
  30.6 2.9 maximum_bitcast_fusion.2
  34.9 1.1 pad_maximum_fusion
  37.7 1.4 fusion.19
  39.0 10.3 %copy.122 = bf16[2,16,16,256]{0,1,3,2:T(8,128)(2,1)} copy(bf16[2,16,16,256]{3,2,1,0:T(8,128)(2,1)S(1)} %fusion.19) | data formatting | bytes 524288 | tf_op jit(solution)/shard_map/convert_element_type | solution.py:47
  49.3 28.6 %gather_fusion.2 = bf16[128,2,256]{1,0,2:T(8,128)(2,1)} fusion(bf16[16,2,4096]{1,0,2:T(8,128)(2,1)} %bitcast.148, s32[128]{0:T(128)S(1)} %reshape.330), kind=kCustom, calls=%fused_computation.2 | custom fusion | bytes 263680 | tf_op jit(solution)/shard_map/vmap(vmap())/gather | solution.py:65
  77.9 11.5 %copy.102 = bf16[16,8,2,256]{3,0,2,1:T(8,128)(2,1)S(1)} copy(bf16[16,8,2,256]{2,1,0,3:T(8,128)(2,1)} %bitcast.153) | data formatting | bytes 262144 | tf_op jit(solution)/shard_map/vmap(vmap())/gather | solution.py:65
  89.6 2.0 fusion.10
  91.7 3.3 copy.103
  95.0 14.8 %fusion.58 = bf16[32,2,256,256]{3,0,2,1:T(8,128)(2,1)} fusion(bf16[8,2,256,256]{3,0,2,1:T(8,128)(2,1)S(1)} %copy.103, s32[8]{0:T(128)S(1)} %add_reduce_fusion, pred[8]{0:T(512)(128)(4,1)S(1)} %dynamic-slice_bitcast_fusion), kind=kOutput, calls=%fused_computation.105 | convolution fusion | flops 67109376 | bytes 10485800 | tf_op jit(solution)/shard_map/mk,kdij->mdij/dot_general | solution.py:149
  109.8 11.4 %copy.104 = bf16[32,2,256,256]{3,2,1,0:T(8,128)(2,1)} copy(bf16[32,2,256,256]{3,0,2,1:T(8,128)(2,1)} %fusion.58) | data formatting | bytes 16777216 | tf_op jit(solution)/shard_map/mk,kdij->mdij/dot_general | solution.py:149
  121.2 9.9 %all-to-all-start = ((bf16[32,2,256,256]{3,2,1,0:T(8,128)(2,1)}), bf16[32,2,256,256]{3,2,1,0:T(8,128)(2,1)}, u32[]{:S(2)}, u32[]{:S(2)}) async-start(bf16[32,2,256,256]{3,2,1,0:T(8,128)(2,1)} %copy.104), calls=%async_computation | async-start | bytes 16777216 | tf_op jit(solution)/shard_map/all_to_all | solution.py:155
  131.0 1.9 gather_fusion.1
  133.4 186.2 %all-to-all-done = bf16[32,2,256,256]{3,2,1,0:T(8,128)(2,1)} async-done(((bf16[32,2,256,256]{3,2,1,0:T(8,128)(2,1)}), bf16[32,2,256,256]{3,2,1,0:T(8,128)(2,1)}, u32[]{:S(2)}, u32[]{:S(2)}) %all-to-all-start) | async-done | bytes 8388640 | tf_op jit(solution)/shard_map/all_to_all | solution.py:155
  319.6 8.1 %fusion.11 = f32[2,4,256,256]{3,1,2,0:T(4,128)S(1)} fusion(bf16[4,32,1,1]{1,0,3,2:T(4,128)(2,1)S(1)} %fusion.24, bf16[32,2,256,256]{3,2,1,0:T(8,128)(2,1)} %all-to-all-done), kind=kOutput, calls=%fused_computation.19 | convolution fusion | flops 33554432 | bytes 10486016 | tf_op jit(solution)/shard_map/lm,mdij->dlij/dot_general | solution.py:152
  328.3 4.8 fusion.25
  333.1 11.4 %copy.108 = bf16[32,2,256,256]{3,2,1,0:T(8,128)(2,1)} copy(bf16[32,2,256,256]{3,0,2,1:T(8,128)(2,1)} %fusion.25) | data formatting | bytes 16777216 | tf_op jit(solution)/shard_map/lm,dlij->mdij/dot_general | solution.py:159
  344.5 20.6 %all-to-all-start.1 = ((bf16[32,2,256,256]{3,2,1,0:T(8,128)(2,1)}), bf16[32,2,256,256]{3,2,1,0:T(8,128)(2,1)}, u32[]{:S(2)}, u32[]{:S(2)}) async-start(bf16[32,2,256,256]{3,2,1,0:T(8,128)(2,1)} %copy.108), calls=%async_computation.1 | async-start | bytes 16777216 | tf_op jit(solution)/shard_map/all_to_all | solution.py:160
  365.1 185.3 %all-to-all-done.1 = bf16[32,2,256,256]{3,2,1,0:T(8,128)(2,1)} async-done(((bf16[32,2,256,256]{3,2,1,0:T(8,128)(2,1)}), bf16[32,2,256,256]{3,2,1,0:T(8,128)(2,1)}, u32[]{:S(2)}, u32[]{:S(2)}) %all-to-all-start.1) | async-done | bytes 8388640 | tf_op jit(solution)/shard_map/all_to_all | solution.py:160
  550.4 8.0 %fusion.14 = bf16[8,2,256,256,1]{3,0,2,1,4:T(8,128)(2,1)S(1)} fusion(bf16[32,2,256,256]{3,2,1,0:T(8,128)(2,1)} %all-to-all-done.1, s32[8]{0:T(128)S(1)} %add_reduce_fusion, pred[8]{0:T(512)(128)(4,1)S(1)} %dynamic-slice_bitcast_fusion), kind=kOutput, calls=%fused_computation.20 | convolution fusion | flops 67109376 | bytes 10485800 | tf_op jit(solution)/shard_map/mk,mdij->kdij/dot_general | solution.py:162
  559.3 15.0 %psum.14 = f32[16]{0:T(128)S(1)} all-reduce(f32[16]{0:T(128)S(1)} %broadcast_multiply_fusion), channel_id=1, replica_groups=mesh['pulse'=32,'band'=8] {'band'}, use_global_device_ids=true, to_apply=%region_2.5 | all-reduce | flops 16 | bytes 128 | tf_op jit(solution)/shard_map/psum | solution.py:166
  575.0 1.7 copy.112
  576.7 84.9 %psum.15 = f32[]{:T(128)} all-reduce(f32[]{:T(128)} %multiply_reduce_fusion), channel_id=1, replica_groups=mesh['pulse'=32,'band'=8] {'pulse'}, use_global_device_ids=true, to_apply=%region_4.7 | all-reduce | flops 1 | bytes 8 | tf_op jit(solution)/shard_map/psum | solution.py:167
  (73 shorter events, 12.8 us)
Async XLA Ops:
  0.6 2.9 copy-start
  2.2 32.6 %collective-permute-start = (bf16[2,16,2048]{2,1,0:T(8,128)(2,1)}, bf16[2,16,2048]{2,1,0:T(8,128)(2,1)}, u32[]{:S(2)}, u32[]{:S(2)}) collective-permute-start(bf16[2,16,2048]{2,1,0:T(8,128)(2,1)} %slice.71), channel_id=1, source_target_pairs={{1,0},{2,1},{3,2},{4,3},{5,4},{6,5},{7,6},{9,8},{10,9},{11,10},{12... | collective-permute-start | bytes 393224 | tf_op jit(solution)/shard_map/ppermute | solution.py:19
  6.4 0.8 copy-start.4
  7.1 3.2 copy-start.6
  30.5 2.9 copy-start.8
  30.5 2.9 copy-start.9
  30.6 2.9 copy-start.11
  30.6 3.0 copy-start.7
  30.6 3.0 copy-start.10
  36.0 1.7 copy-start.3
  121.2 9.9 %copy-start.2 = (s32[128]{0:T(128)S(1)}, s32[128]{0:T(128)}, u32[]{:S(2)}) copy-start(s32[128]{0:T(128)} %param.14) | copy-start | bytes 1540
  121.2 198.4 %all-to-all-start = ((bf16[32,2,256,256]{3,2,1,0:T(8,128)(2,1)}), bf16[32,2,256,256]{3,2,1,0:T(8,128)(2,1)}, u32[]{:S(2)}, u32[]{:S(2)}) async-start(bf16[32,2,256,256]{3,2,1,0:T(8,128)(2,1)} %copy.104), calls=%async_computation | async-start | bytes 16777216 | tf_op jit(solution)/shard_map/all_to_all | solution.py:155
  131.0 1.9 copy-start.5
  344.5 205.9 %all-to-all-start.1 = ((bf16[32,2,256,256]{3,2,1,0:T(8,128)(2,1)}), bf16[32,2,256,256]{3,2,1,0:T(8,128)(2,1)}, u32[]{:S(2)}, u32[]{:S(2)}) async-start(bf16[32,2,256,256]{3,2,1,0:T(8,128)(2,1)} %copy.108), calls=%async_computation.1 | async-start | bytes 16777216 | tf_op jit(solution)/shard_map/all_to_all | solution.py:160
  558.4 104.4 %copy-start.1 = (f32[3,512]{1,0:T(4,128)S(1)}, f32[3,512]{1,0:T(4,128)}, u32[]{:S(2)}) copy-start(f32[3,512]{1,0:T(4,128)} %param.12) | copy-start | bytes 18436
where the time goes:
time: 672 us; the launch traced here: 663 us
  waiting for transfers between devices  371 us (55%)
  local copies, waits for them, and re-layouts  104 us (15%)
  blocking collectives  99.9 us (15%)
  matrix products  40.1 us (6%)
  starting transfers between devices  31.7 us (5%)
  other arithmetic  13.6 us (2%)
    all_to_all x1, waiting for transfers between devices, on_device(): lax.all_to_all(outgoing, 'pulse', split_axis=0, concat_axis=0, tiled=True)  186 us
    all_to_all x1, waiting for transfers between devices, on_device(): lax.all_to_all(returned, 'pulse', split_axis=0, concat_axis=0, tiled=True)  185 us
    psum x1, blocking collectives, on_device(): square_sum = lax.psum(jnp.sum(band_grad * band_grad), 'pulse')  84.9 us
    gather x4, local copies, waits for them, and re-layouts, per_slot(): return lax.dynamic_slice_in_dim(series, first_index, TILE, 1)  40.3 us
    all_to_all x1, starting transfers between devices, on_device(): lax.all_to_all(returned, 'pulse', split_axis=0, concat_axis=0, tiled=True)  20.6 us
    psum x1, blocking collectives, on_device(): band_grad = lax.psum(local_grad, 'band')  15 us
    dot_general x1, matrix products, on_device(): jnp.einsum('mk,kdij->mdij', send_map, partial_value, preferred_element_ty...  14.8 us
  transfers between devices with their start and end apart: 3, of which 2 were waited for; matrix products, arithmetic and copies ran while one was open for 5% of the time, Pallas kernels for 0%

commit v1 on v0

v1 whole, which is shorter than its diff:
```python
import math

import jax
import jax.numpy as jnp
from jax import lax
from jax.experimental import pallas as pl
from jax.experimental.pallas import tpu as pltpu
from jax.sharding import PartitionSpec as P

TILE = 256
TAPS = 2048
RB = 4096
P_DEV = 16
FOOT = 8
TILES_DEV = 4
NTILE = 128
PULSES = 512
N_PULSE = 32
N_BAND = 8
LANE = 128

SPANS = TAPS // TILE + 1
BLOCKS = RB // TILE
ROWS = BLOCKS * P_DEV
KDIM = 2 * PULSES
FACTOR = 0.5 / math.sqrt(P_DEV)

NT = (((1,), (1,)), ((), ()))
NN = (((1,), (0,)), ((), ()))

VMEM_BYTES = 48 * 1024 * 1024


def vmem():
    return pl.BlockSpec(memory_space=pltpu.VMEM)


def smem():
    return pl.BlockSpec(memory_space=pltpu.SMEM)


def taps_kernel(replica_ref, taps_ref):
    width = TAPS + LANE
    chunks = width // LANE
    sub = lax.broadcasted_iota(jnp.int32, (8, width), 0)
    zero = jnp.zeros((16, LANE), jnp.bfloat16)
    for comp in range(2):
        line = replica_ref[comp : comp + 1, :].astype(jnp.float32)
        line = jnp.concatenate([line, jnp.zeros((1, LANE), jnp.float32)], axis=1)
        wide = jnp.broadcast_to(line, (8, width))
        base = wide
        for r in range(1, 8):
            base = jnp.where(sub == r, pltpu.roll(wide, r, 1), base)
        for j in range(8):
            first = base if j == 0 else pltpu.roll(base, 16 * j, 1)
            pair = jnp.concatenate([first, pltpu.roll(base, 16 * j + 8, 1)], axis=0)
            pair = pair.astype(jnp.bfloat16)
            for half in range(2):
                row = LANE * half + 16 * j
                for c in range(2 * SPANS):
                    src = c - half
                    piece = pair[:, LANE * src : LANE * src + LANE] if 0 <= src < chunks else zero
                    col = 512 * (c // 2) + TILE * comp + LANE * (c % 2)
                    taps_ref[row : row + 16, col : col + LANE] = piece


def lane_shift(low, high, shift):
    first, second = low[:, :LANE], low[:, LANE:]
    third, fourth = high[:, :LANE], high[:, LANE:]
    far = shift >= LANE
    parts = [
        jnp.where(far, second, first),
        jnp.where(far, third, second),
        jnp.where(far, fourth, third),
    ]
    step = shift & (LANE - 1)
    lane = lax.broadcasted_iota(jnp.int32, first.shape, 1)
    index = (lane + step) & (LANE - 1)
    turned = [jnp.take_along_axis(part, index, axis=1) for part in parts]
    stay = lane < LANE - step
    return jnp.concatenate(
        [jnp.where(stay, turned[0], turned[1]), jnp.where(stay, turned[1], turned[2])], axis=1
    )


def rows_kernel(
    footprint_ref, slot_ref, echo_ref, tail_ref, taps_ref, angle_ref, offset_ref, out_ref, win_ref
):
    me = lax.axis_index("pulse")
    for n in range(BLOCKS + SPANS - 1):
        for comp in range(2):
            if n < BLOCKS:
                piece = echo_ref[comp, :, TILE * n : TILE * n + TILE]
            else:
                piece = tail_ref[comp, :, TILE * (n - BLOCKS) : TILE * (n - BLOCKS) + TILE]
            win_ref[P_DEV * n : P_DEV * n + P_DEV, TILE * comp : TILE * comp + TILE] = piece
            if comp == 0:
                win_ref[P_DEV * n : P_DEV * n + P_DEV, 2 * TILE :] = -piece
    total = jnp.zeros((2 * ROWS, TILE), jnp.float32)
    for a in range(SPANS):
        rows = slice(P_DEV * a, P_DEV * a + ROWS)
        left = jnp.concatenate([win_ref[rows, : 2 * TILE], win_ref[rows, TILE:]], axis=0)
        total += lax.dot_general(
            left, taps_ref[:, 512 * a : 512 * a + 512], NT, preferred_element_type=jnp.float32
        )
    series = jnp.concatenate([total[:ROWS], total[ROWS:]], axis=1).astype(jnp.bfloat16)

    begin = pl.multiple_of(me * P_DEV, P_DEV)
    offsets = offset_ref[pl.ds(begin, P_DEV), :]
    pulse = lax.broadcasted_iota(jnp.int32, (P_DEV, ROWS), 0)
    lane = lax.broadcasted_iota(jnp.int32, (P_DEV, ROWS), 1)
    low_hot, high_hot = [], []
    for k in range(FOOT):
        block = offsets[:, k : k + 1] >> 8
        low_hot.append(jnp.where(lane == block * P_DEV + pulse, 1.0, 0.0))
        block = jnp.minimum(block + 1, BLOCKS - 1)
        high_hot.append(jnp.where(lane == block * P_DEV + pulse, 1.0, 0.0))
    hot = jnp.concatenate(low_hot + high_hot, axis=0).astype(jnp.bfloat16)
    picked = lax.dot_general(hot, series, NN, preferred_element_type=jnp.float32)

    wide_lane = lax.broadcasted_iota(jnp.int32, (P_DEV, PULSES), 1)
    wide_sub = lax.broadcasted_iota(jnp.int32, (P_DEV, PULSES), 0)
    mine = wide_lane == begin + wide_sub
    kappa = jnp.sum(jnp.where(mine, angle_ref[1:2, :], 0.0), axis=1, keepdims=True)
    phase = jnp.sum(jnp.where(mine, angle_ref[2:3, :], 0.0), axis=1, keepdims=True)
    column = lax.broadcasted_iota(jnp.int32, (P_DEV, LANE), 1)
    tiles = [footprint_ref[me, k] for k in range(FOOT)]
    tile_row = jnp.zeros((P_DEV, LANE), jnp.float32)
    for k in range(FOOT):
        tile_row = jnp.where(column == k, jnp.maximum(tiles[k], 0).astype(jnp.float32), tile_row)
    turn = kappa * tile_row + phase
    cosine, sine = jnp.cos(turn), jnp.sin(turn)

    out_ref[...] = jnp.zeros_like(out_ref)
    for k in range(FOOT):
        low = picked[P_DEV * k : P_DEV * k + P_DEV]
        high = picked[P_DEV * (FOOT + k) : P_DEV * (FOOT + k) + P_DEV]
        shift = jnp.broadcast_to(offsets[:, k : k + 1] & (TILE - 1), (P_DEV, LANE))
        real = lane_shift(low[:, :TILE], high[:, :TILE], shift)
        imag = lane_shift(low[:, TILE:], high[:, TILE:], shift)
        c, s = cosine[:, k : k + 1], sine[:, k : k + 1]
        rot_real = ((real * c - imag * s) * FACTOR).astype(jnp.bfloat16)
        rot_imag = ((real * s + imag * c) * FACTOR).astype(jnp.bfloat16)
        owner = slot_ref[jnp.maximum(tiles[k], 0)] >> 2

        @pl.when(tiles[k] >= 0)
        def _():
            out_ref[owner, 0] = rot_real
            out_ref[owner, 1] = rot_imag


def steer_kernel(footprint_ref, slot_ref, angle_ref, steer_ref, local_ref):
    me = lax.axis_index("pulse")

    def per_block(d, carry):
        found = jnp.int32(-1)
        for k in range(FOOT):
            tile = footprint_ref[d, k]
            slot = slot_ref[jnp.maximum(tile, 0)]
            found = jnp.where((tile >= 0) & ((slot >> 2) == me), slot & 3, found)
        local_ref[d] = found
        return carry

    lax.fori_loop(0, N_PULSE, per_block, 0)

    def per_rows(g, carry):
        begin = pl.multiple_of(g * 16, 16)
        j = (begin + lax.broadcasted_iota(jnp.int32, (16, PULSES), 0)).astype(jnp.float32)
        phases = j * angle_ref[0:1, :]
        cosine = jnp.cos(phases).astype(jnp.bfloat16)
        sine = jnp.sin(phases).astype(jnp.bfloat16)
        steer_ref[pl.ds(begin, 16), :PULSES] = cosine
        steer_ref[pl.ds(begin, 16), PULSES:] = -sine
        lower = pl.multiple_of(TILE + g * 16, 16)
        steer_ref[pl.ds(lower, 16), :PULSES] = sine
        steer_ref[pl.ds(lower, 16), PULSES:] = cosine
        return carry

    lax.fori_loop(0, TILE // 16, per_rows, 0)


def owner_kernel(local_ref, arrived_ref, steer_ref, image_ref, grad_ref, rows_ref, weight_ref):
    for d in range(N_PULSE):
        slot = local_ref[d]
        for comp in range(2):
            piece = arrived_ref[d, comp]
            row = PULSES * comp + P_DEV * d
            for l in range(TILES_DEV):
                rows_ref[row : row + P_DEV, TILE * l : TILE * l + TILE] = jnp.where(
                    slot == l, piece, jnp.zeros_like(piece)
                )
    for l in range(TILES_DEV):
        cols = slice(TILE * l, TILE * l + TILE)
        total = lax.dot_general(
            steer_ref[...], rows_ref[:, cols], NN, preferred_element_type=jnp.float32
        )
        image_ref[:, cols] = total
        real, imag = total[:TILE], total[TILE:]
        power = real * real + imag * imag
        weight_ref[:TILE, cols] = (-power * imag).astype(jnp.bfloat16)
        weight_ref[TILE:, cols] = (power * real).astype(jnp.bfloat16)
    sums = []
    for h in range(KDIM // TILE):
        cols = slice(TILE * h, TILE * h + TILE)
        back = lax.dot_general(
            weight_ref[...], rows_ref[cols, :], NT, preferred_element_type=jnp.float32
        )
        sums.append(
            jnp.sum(back * steer_ref[:, cols].astype(jnp.float32), axis=0, keepdims=True)
        )
    halves = [-4.0 * (sums[h] + sums[h + 2]) for h in range(2)]
    for c in range(PULSES // LANE):
        piece = halves[c // 2][:, LANE * (c % 2) : LANE * (c % 2) + LANE]
        for b in range(N_BAND):
            grad_ref[b, c : c + 1, :] = piece


def image_kernel(flat_ref, out_ref):
    out_ref[0, 0] = flat_ref[...].T


def params():
    return pltpu.CompilerParams(vmem_limit_bytes=VMEM_BYTES)


def on_device(echoes, replica, pulse_angles, footprint, tile_slot, offsets):
    me = lax.axis_index("pulse")
    pairs = [(i, i - 1) for i in range(1, N_BAND)]
    tail = lax.ppermute(echoes, "band", pairs)
    taps = pl.pallas_call(
        taps_kernel,
        out_shape=jax.ShapeDtypeStruct((TILE, 2 * TILE * SPANS), jnp.bfloat16),
        in_specs=[vmem()],
        out_specs=vmem(),
        compiler_params=params(),
        cost_estimate=pl.CostEstimate(flops=0, bytes_accessed=8 << 20, transcendentals=0),
        name="taps",
    )(replica)
    rows = pl.pallas_call(
        rows_kernel,
        grid=(1,),
        out_shape=jax.ShapeDtypeStruct((N_PULSE, 2, P_DEV, TILE), jnp.bfloat16),
        in_specs=[
            smem(),
            smem(),
            vmem(),
            pl.BlockSpec((2, P_DEV, TAPS), lambda g: (0, 0, 0)),
            vmem(),
            vmem(),
            vmem(),
        ],
        out_specs=vmem(),
        scratch_shapes=[pltpu.VMEM((ROWS + P_DEV * (SPANS - 1), 3 * TILE), jnp.bfloat16)],
        compiler_params=params(),
        name="rows",
    )(footprint, tile_slot, echoes, tail, taps, pulse_angles, offsets)
    steer, local = pl.pallas_call(
        steer_kernel,
        out_shape=[
            jax.ShapeDtypeStruct((2 * TILE, KDIM), jnp.bfloat16),
            jax.ShapeDtypeStruct((N_PULSE,), jnp.int32),
        ],
        in_specs=[smem(), smem(), vmem()],
        out_specs=[vmem(), smem()],
        compiler_params=params(),
        cost_estimate=pl.CostEstimate(flops=0, bytes_accessed=20 << 20, transcendentals=0),
        name="steer",
    )(footprint, tile_slot, pulse_angles)
    arrived = lax.all_to_all(rows, "pulse", split_axis=0, concat_axis=0, tiled=True)
    image_flat, grad = pl.pallas_call(
        owner_kernel,
        out_shape=[
            jax.ShapeDtypeStruct((2 * TILE, TILES_DEV * TILE), jnp.float32),
            jax.ShapeDtypeStruct((N_BAND, PULSES // LANE, LANE), jnp.float32),
        ],
        in_specs=[smem(), vmem(), vmem()],
        out_specs=[vmem(), vmem()],
        scratch_shapes=[
            pltpu.VMEM((KDIM, TILES_DEV * TILE), jnp.bfloat16),
            pltpu.VMEM((2 * TILE, TILES_DEV * TILE), jnp.bfloat16),
        ],
        compiler_params=params(),
        name="owner",
    )(local, arrived, steer)
    image = pl.pallas_call(
        image_kernel,
        grid=(2, TILES_DEV),
        out_shape=jax.ShapeDtypeStruct((2, TILES_DEV, TILE, TILE), jnp.float32),
        in_specs=[pl.BlockSpec((TILE, TILE), lambda c, l: (c, l))],
        out_specs=pl.BlockSpec((1, 1, TILE, TILE), lambda c, l: (c, l, 0, 0)),
        compiler_params=params(),
        name="image",
    )(image_flat)
    band_all = lax.all_to_all(grad, "band", split_axis=0, concat_axis=0, tiled=True)
    band_sum = jnp.sum(band_all, axis=0, keepdims=True)
    spread = jnp.broadcast_to(band_sum, (N_PULSE, PULSES // LANE, LANE))
    pulse_all = lax.all_to_all(spread, "pulse", split_axis=0, concat_axis=0, tiled=True)
    gradient = jnp.sum(pulse_all, axis=0)
    scaled = gradient / jnp.sqrt(jnp.sum(gradient * gradient) / PULSES + 1e-05)
    phase_gradient = lax.dynamic_slice_in_dim(scaled.reshape(PULSES), me * P_DEV, P_DEV, 0)
    return (image, phase_gradient)


def solution(mesh):
    placed = (P(None, "pulse", "band"), P(), P(), P(), P(), P())
    return jax.shard_map(
        on_device,
        mesh=mesh,
        in_specs=placed,
        out_specs=(P(None, "pulse", "band", None), P("pulse")),
        check_vma=False,
    )
```

time: 672 us -> 72.4 us (0.11)
  the two profiles are of different devices: /device:TPU:128 before, /device:TPU:1 now
where the time goes in v1:
time: 72.4 us; the launch traced here: 71.9 us
  starting transfers between devices  21.1 us (29%)
  Pallas kernels  16.4 us (23%)
  waiting for transfers between devices  16.4 us (23%)
  blocking collectives  10.9 us (15%)
  local copies, waits for them, and re-layouts  5.06 us (7%)
  between operations  1.43 us (2%)
    all_to_all x1, starting transfers between devices, on_device(): lax.all_to_all(rows, 'pulse', split_axis=0, concat_axis=0, tiled=True)  11 us
    all_to_all x1, blocking collectives, on_device(): lax.all_to_all(grad, 'band', split_axis=0, concat_axis=0, tiled=True)  10.9 us
    all_to_all x1, waiting for transfers between devices, on_device(): lax.all_to_all(rows, 'pulse', split_axis=0, concat_axis=0, tiled=True)  9.77 us
    ppermute x1, starting transfers between devices, on_device(): tail = lax.ppermute(echoes, 'band', pairs)  5.28 us
    all_to_all x1, waiting for transfers between devices, on_device(): lax.all_to_all(spread, 'pulse', split_axis=0, concat_axis=0, tiled=True)  5.2 us
    all_to_all x1, starting transfers between devices, on_device(): lax.all_to_all(spread, 'pulse', split_axis=0, concat_axis=0, tiled=True)  4.76 us
    pallas_call x1, Pallas kernels, on_device(): pl.pallas_call(steer_kernel, out_shape=[jax.ShapeDtypeStruct((2 * TILE, K...  4.58 us
    pallas_call x1, Pallas kernels, on_device(): pl.pallas_call(rows_kernel, grid=(1,), out_shape=jax.ShapeDtypeStruct((N_...  4.53 us
  transfers between devices with their start and end apart: 3, of which 3 were waited for; matrix products, arithmetic and copies ran while one was open for 1% of the time, Pallas kernels for 12%

profile of v1, /device:TPU:1, one launch (start us, length us, event | category | flops | bytes accessed | tf_op | source)
XLA Modules:
  0.0 71.9 jit_solution(2908164055836652098)
XLA Ops:
  0.6 0.0 copy-start.2
  0.6 0.0 copy-start.3
  0.6 5.3 %collective-permute-start = (bf16[2,16,4096]{2,1,0:T(8,128)(2,1)}, bf16[2,16,4096]{2,1,0:T(8,128)(2,1)S(1)}, u32[]{:S(2)}, u32[]{:S(2)}) collective-permute-start(bf16[2,16,4096]{2,1,0:T(8,128)(2,1)} %echo_ref.1), channel_id=1, source_target_pairs={{1,0},{2,1},{3,2},{4,3},{5,4},{6,5},{7,6},{9,8},{10,9},{11,10},{12... | collective-permute-start | bytes 786440 | tf_op jit(solution)/shard_map/ppermute | solution.py:229
  5.9 0.8 %copy.14.footprint_ref = s32[32,8]{1,0:T(8,128)S(1)} copy(s32[32,8]{0,1:T(8,128)} %param.9) | data formatting | bytes 2048 | tf_op args[3]
  6.7 0.0 copy-start.4
  6.7 0.7 copy-done.4
  7.4 0.0 copy-start.6
  7.4 0.0 copy-start.5
  7.4 0.6 taps.1.taps_ref
  8.1 0.1 copy-done.6
  8.1 0.1 copy.16.offset_ref
  8.2 1.4 %collective-permute-done.tail_ref = bf16[2,16,4096]{2,1,0:T(8,128)(2,1)S(1)} collective-permute-done((bf16[2,16,4096]{2,1,0:T(8,128)(2,1)}, bf16[2,16,4096]{2,1,0:T(8,128)(2,1)S(1)}, u32[]{:S(2)}, u32[]{:S(2)}) %collective-permute-start) | collective-permute-done | bytes 262176 | tf_op jit(solution)/shard_map/ppermute | solution.py:229
  9.6 0.0 copy-done.2
  9.6 0.0 copy-done.3
  9.6 0.0 copy-done.5
  9.6 4.5 %rows.1 = bf16[32,2,16,256]{3,2,1,0:T(8,128)(2,1)} custom-call(s32[32,8]{1,0:T(8,128)S(1)} %copy.14.footprint_ref, s32[128]{0:T(128)S(1)} %copy-done.5, bf16[2,16,4096]{2,1,0:T(8,128)(2,1)S(1)} %copy-done.2, bf16[2,16,4096]{2,1,0:T(8,128)(2,1)S(1)} %collective-permute-done.tail_ref, bf16[256,4608]{1,0:T(8,128)(2,1)S(1)} %taps.1.taps_ref, ...), custom_call_target="tpu_custom_call" | custom-call | tf_op jit(solution)/shard_map/rows/pallas_call | solution.py:239
  14.2 11.0 %all-to-all-start = ((bf16[32,2,16,256]{3,2,1,0:T(8,128)(2,1)}), bf16[32,2,16,256]{3,2,1,0:T(8,128)(2,1)S(1)}, u32[]{:S(2)}, u32[]{:S(2)}) async-start(bf16[32,2,16,256]{3,2,1,0:T(8,128)(2,1)} %rows.1), calls=%async_computation | async-start | bytes 1048576 | tf_op jit(solution)/shard_map/all_to_all | solution.py:269
  25.2 4.6 %steer.1 = (bf16[512,1024]{1,0:T(8,128)(2,1)S(1)}, s32[32]{0:T(128)S(1)}) custom-call(s32[32,8]{1,0:T(8,128)S(1)} %copy.14.footprint_ref, s32[128]{0:T(128)S(1)} %copy-done.5, f32[3,512]{1,0:T(4,128)S(1)} %copy-done.3), custom_call_target="tpu_custom_call" | custom-call | bytes 20971520 | tf_op jit(solution)/shard_map/steer/pallas_call | solution.py:257
  29.8 0.0 copy-start
  29.8 1.0 %copy-done = bf16[512,1024]{1,0:T(8,128)(2,1)} copy-done((bf16[512,1024]{1,0:T(8,128)(2,1)}, bf16[512,1024]{1,0:T(8,128)(2,1)S(1)}, u32[]{:S(2)}) %copy-start) | copy-done | bytes 1048600
  30.8 9.8 %all-to-all-done.arrived_ref = bf16[32,2,16,256]{3,2,1,0:T(8,128)(2,1)S(1)} async-done(((bf16[32,2,16,256]{3,2,1,0:T(8,128)(2,1)}), bf16[32,2,16,256]{3,2,1,0:T(8,128)(2,1)S(1)}, u32[]{:S(2)}, u32[]{:S(2)}) %all-to-all-start) | async-done | bytes 524320 | tf_op jit(solution)/shard_map/all_to_all | solution.py:269
  40.6 0.0 copy-start.1
  40.6 1.2 %copy-done.1 = bf16[512,1024]{1,0:T(8,128)(2,1)S(1)} copy-done((bf16[512,1024]{1,0:T(8,128)(2,1)S(1)}, bf16[512,1024]{1,0:T(8,128)(2,1)}, u32[]{:S(2)}) %copy-start.1) | copy-done | bytes 1048600
  41.8 3.0 %owner.1 = (f32[512,1024]{1,0:T(8,128)S(1)}, f32[8,4,128]{2,1,0:T(4,128)S(1)}) custom-call(s32[32]{0:T(128)S(1)} %get-tuple-element.6.local_ref, bf16[32,2,16,256]{3,2,1,0:T(8,128)(2,1)S(1)} %all-to-all-done.arrived_ref, bf16[512,1024]{1,0:T(8,128)(2,1)S(1)} %copy-done.1), custom_call_target="tpu_custom_call" | custom-call | tf_op jit(solution)/shard_map/owner/pallas_call | solution.py:270
  44.8 10.9 %all_to_all.15 = f32[8,4,128]{2,1,0:T(4,128)S(1)} all-to-all(f32[8,4,128]{2,1,0:T(4,128)S(1)} %get-tuple-element.9), channel_id=1, replica_groups=mesh['pulse'=32,'band'=8] {'band'}, dimensions={0} | all-to-all | bytes 32768 | tf_op jit(solution)/shard_map/all_to_all | solution.py:294
  55.7 0.6 broadcast_in_dim.2
  56.3 4.8 %all-to-all-start.2 = ((f32[32,4,128]{2,1,0:T(4,128)}), f32[32,4,128]{2,1,0:T(4,128)S(1)}, u32[]{:S(2)}, u32[]{:S(2)}) async-start(f32[32,4,128]{2,1,0:T(4,128)} %broadcast_in_dim.2), calls=%async_computation.2 | async-start | bytes 131072 | tf_op jit(solution)/shard_map/all_to_all | solution.py:297
  61.1 3.6 %image.1 = f32[2,4,256,256]{3,2,1,0:T(8,128)} custom-call(f32[512,1024]{1,0:T(8,128)S(1)} %get-tuple-element.8.flat_ref), custom_call_target="tpu_custom_call" | custom-call | tf_op jit(solution)/shard_map/image/pallas_call | solution.py:285
  64.7 5.2 %all-to-all-done.2 = f32[32,4,128]{2,1,0:T(4,128)S(1)} async-done(((f32[32,4,128]{2,1,0:T(4,128)}), f32[32,4,128]{2,1,0:T(4,128)S(1)}, u32[]{:S(2)}, u32[]{:S(2)}) %all-to-all-start.2) | async-done | bytes 65568 | tf_op jit(solution)/shard_map/all_to_all | solution.py:297
  70.0 0.6 multiply_reduce_fusion
  71.3 0.6 dynamic_slice.3
  (3 shorter events, 0.1 us)
Async XLA Ops:
  0.6 9.0 %copy-start.2 = (bf16[2,16,4096]{2,1,0:T(8,128)(2,1)S(1)}, bf16[2,16,4096]{2,1,0:T(8,128)(2,1)}, u32[]{:S(2)}) copy-start(bf16[2,16,4096]{2,1,0:T(8,128)(2,1)} %echo_ref.1) | copy-start | bytes 786436
  0.6 9.0 %copy-start.3 = (f32[3,512]{1,0:T(4,128)S(1)}, f32[3,512]{1,0:T(4,128)}, u32[]{:S(2)}) copy-start(f32[3,512]{1,0:T(4,128)} %angle_ref.3) | copy-start | bytes 18436
  0.6 9.0 %collective-permute-start = (bf16[2,16,4096]{2,1,0:T(8,128)(2,1)}, bf16[2,16,4096]{2,1,0:T(8,128)(2,1)S(1)}, u32[]{:S(2)}, u32[]{:S(2)}) collective-permute-start(bf16[2,16,4096]{2,1,0:T(8,128)(2,1)} %echo_ref.1), channel_id=1, source_target_pairs={{1,0},{2,1},{3,2},{4,3},{5,4},{6,5},{7,6},{9,8},{10,9},{11,10},{12... | collective-permute-start | bytes 786440 | tf_op jit(solution)/shard_map/ppermute | solution.py:229
  6.7 0.7 copy-start.4
  7.4 0.7 copy-start.6
  7.4 2.2 %copy-start.5 = (s32[128]{0:T(128)S(1)}, s32[128]{0:T(128)}, u32[]{:S(2)}) copy-start(s32[128]{0:T(128)} %slot_ref.3) | copy-start | bytes 1540
  14.2 26.4 %all-to-all-start = ((bf16[32,2,16,256]{3,2,1,0:T(8,128)(2,1)}), bf16[32,2,16,256]{3,2,1,0:T(8,128)(2,1)S(1)}, u32[]{:S(2)}, u32[]{:S(2)}) async-start(bf16[32,2,16,256]{3,2,1,0:T(8,128)(2,1)} %rows.1), calls=%async_computation | async-start | bytes 1048576 | tf_op jit(solution)/shard_map/all_to_all | solution.py:269
  29.8 1.0 %copy-start = (bf16[512,1024]{1,0:T(8,128)(2,1)}, bf16[512,1024]{1,0:T(8,128)(2,1)S(1)}, u32[]{:S(2)}) copy-start(bf16[512,1024]{1,0:T(8,128)(2,1)S(1)} %get-tuple-element.7.steer_ref) | copy-start | bytes 3145732
  40.6 1.2 %copy-start.1 = (bf16[512,1024]{1,0:T(8,128)(2,1)S(1)}, bf16[512,1024]{1,0:T(8,128)(2,1)}, u32[]{:S(2)}) copy-start(bf16[512,1024]{1,0:T(8,128)(2,1)} %copy-done) | copy-start | bytes 3145732
  56.3 13.6 %all-to-all-start.2 = ((f32[32,4,128]{2,1,0:T(4,128)}), f32[32,4,128]{2,1,0:T(4,128)S(1)}, u32[]{:S(2)}, u32[]{:S(2)}) async-start(f32[32,4,128]{2,1,0:T(4,128)} %broadcast_in_dim.2), calls=%async_computation.2 | async-start | bytes 131072 | tf_op jit(solution)/shard_map/all_to_all | solution.py:297

commit v2 on v1

v2 whole, which is shorter than its diff:
```python
import math

import jax
import jax.numpy as jnp
from jax import lax
from jax.experimental import pallas as pl
from jax.experimental.pallas import tpu as pltpu
from jax.sharding import PartitionSpec as P

TILE = 256
TAPS = 2048
RB = 4096
P_DEV = 16
FOOT = 8
TILES_DEV = 4
NTILE = 128
PULSES = 512
N_PULSE = 32
N_BAND = 8
LANE = 128

SPANS = TAPS // TILE + 1
BLOCKS = RB // TILE
ROWS = BLOCKS * P_DEV
KDIM = 2 * PULSES
FACTOR = 0.5 / math.sqrt(P_DEV)

NT = (((1,), (1,)), ((), ()))
NN = (((1,), (0,)), ((), ()))

VMEM_BYTES = 24 * 1024 * 1024


def taps_kernel(replica_ref, taps_ref):
    width = TAPS + LANE
    chunks = width // LANE
    sub = lax.broadcasted_iota(jnp.int32, (8, width), 0)
    zero = jnp.zeros((16, LANE), jnp.bfloat16)
    for comp in range(2):
        line = replica_ref[comp : comp + 1, :].astype(jnp.float32)
        line = jnp.concatenate([line, jnp.zeros((1, LANE), jnp.float32)], axis=1)
        wide = jnp.broadcast_to(line, (8, width))
        base = wide
        for r in range(1, 8):
            base = jnp.where(sub == r, pltpu.roll(wide, r, 1), base)
        for j in range(8):
            first = base if j == 0 else pltpu.roll(base, 16 * j, 1)
            pair = jnp.concatenate([first, pltpu.roll(base, 16 * j + 8, 1)], axis=0)
            pair = pair.astype(jnp.bfloat16)
            for half in range(2):
                row = LANE * half + 16 * j
                for c in range(2 * SPANS):
                    src = c - half
                    piece = pair[:, LANE * src : LANE * src + LANE] if 0 <= src < chunks else zero
                    col = 512 * (c // 2) + TILE * comp + LANE * (c % 2)
                    taps_ref[row : row + 16, col : col + LANE] = piece


def fill_steer(angle_ref, steer_ref):
    step = lax.broadcasted_iota(jnp.int32, (16, PULSES), 0).astype(jnp.float32)
    omega = angle_ref[0:1, :]
    fine, coarse = step * omega, (16.0 * step) * omega
    fine_cos, fine_sin = jnp.cos(fine), jnp.sin(fine)
    coarse_cos, coarse_sin = jnp.cos(coarse), jnp.sin(coarse)
    for a in range(TILE // 16):
        ca, sa = coarse_cos[a : a + 1], coarse_sin[a : a + 1]
        cosine = (fine_cos * ca - fine_sin * sa).astype(jnp.bfloat16)
        sine = (fine_sin * ca + fine_cos * sa).astype(jnp.bfloat16)
        upper, lower = slice(16 * a, 16 * a + 16), slice(TILE + 16 * a, TILE + 16 * a + 16)
        steer_ref[upper, :PULSES] = cosine
        steer_ref[upper, PULSES:] = -sine
        steer_ref[lower, :PULSES] = sine
        steer_ref[lower, PULSES:] = cosine


def own_lanes():
    lane = lax.broadcasted_iota(jnp.int32, (P_DEV, PULSES), 1)
    sub = lax.broadcasted_iota(jnp.int32, (P_DEV, PULSES), 0)
    return lane == lax.axis_index("pulse") * P_DEV + sub


def prep_kernel(
    taps_ref,
    echo_ref,
    angle_ref,
    footprint_ref,
    slot_ref,
    offset_ref,
    steer_ref,
    slots_ref,
    local_ref,
    hot_ref,
    shift_ref,
    turn_ref,
    near_ref,
    win_ref,
    listed_ref,
):
    me = lax.axis_index("pulse")
    fill_steer(angle_ref, steer_ref)

    for n in range(BLOCKS):
        rows = slice(P_DEV * n, P_DEV * n + P_DEV)
        real = echo_ref[0, :, TILE * n : TILE * n + TILE]
        win_ref[rows, :TILE] = real
        win_ref[rows, TILE : 2 * TILE] = echo_ref[1, :, TILE * n : TILE * n + TILE]
        win_ref[rows, 2 * TILE :] = -real
    win_ref[ROWS:, :] = jnp.zeros((P_DEV * (SPANS - 1), 3 * TILE), jnp.bfloat16)
    correlate(win_ref, taps_ref, near_ref, 0, 0, None)

    listed = jnp.concatenate([footprint_ref[...], jnp.full((FOOT, LANE - N_PULSE), -1)], axis=1)
    listed = listed.T
    listed_ref[...] = listed
    lane = lax.broadcasted_iota(jnp.int32, (N_PULSE, LANE), 1)
    slots = jnp.zeros((N_PULSE, LANE), jnp.int32)
    local = jnp.zeros((N_PULSE, 1), jnp.int32)
    for k in range(FOOT):
        same = listed[:N_PULSE, k : k + 1] == lane
        slot = jnp.sum(jnp.where(same, slot_ref[...] + 1, 0), axis=1, keepdims=True)
        slots = jnp.where(lane == k, slot, slots)
        owned = (slot > 0) & (((slot - 1) >> 2) == me)
        local = jnp.where(owned, ((slot - 1) & 3) + 1, local)
    slots_ref[...] = slots
    local_ref[...] = jnp.broadcast_to(local, (N_PULSE, LANE))

    mine = own_lanes()
    tiles = jnp.maximum(listed_ref[pl.ds(me, 1), :], 0).astype(jnp.float32)
    kappa = jnp.sum(jnp.where(mine, angle_ref[1:2, :], 0.0), axis=1, keepdims=True)
    phase = jnp.sum(jnp.where(mine, angle_ref[2:3, :], 0.0), axis=1, keepdims=True)
    turn = kappa * tiles + phase
    cosine, sine = jnp.cos(turn), jnp.sin(turn)
    pulse = lax.broadcasted_iota(jnp.int32, (P_DEV, ROWS), 0)
    pick = lax.broadcasted_iota(jnp.int32, (P_DEV, ROWS), 1)
    low_hot, high_hot = [], []
    for k in range(FOOT):
        rows = slice(P_DEV * k, P_DEV * k + P_DEV)
        offset = jnp.sum(jnp.where(mine, offset_ref[k : k + 1, :], 0), axis=1, keepdims=True)
        block = offset >> 8
        low_hot.append(jnp.where(pick == block * P_DEV + pulse, 1.0, 0.0))
        block = jnp.minimum(block + 1, BLOCKS - 1)
        high_hot.append(jnp.where(pick == block * P_DEV + pulse, 1.0, 0.0))
        shift_ref[rows, :] = jnp.broadcast_to(offset & (TILE - 1), (P_DEV, LANE))
        turn_ref[0, rows, :] = jnp.broadcast_to(cosine[:, k : k + 1], (P_DEV, LANE))
        turn_ref[1, rows, :] = jnp.broadcast_to(sine[:, k : k + 1], (P_DEV, LANE))
    hot_ref[...] = jnp.concatenate(low_hot + high_hot, axis=0).astype(jnp.bfloat16)


def correlate(win_ref, taps_ref, out_ref, first_row, first_span, add_ref):
    count = out_ref.shape[1]
    spans = range(first_span, SPANS)
    taps = taps_ref[:, 512 * first_span :]
    for comp in range(2):
        cols = slice(TILE * comp, TILE * comp + 2 * TILE)
        left = [
            win_ref[first_row + P_DEV * a : first_row + P_DEV * a + count, cols] for a in spans
        ]
        total = lax.dot_general(
            jnp.concatenate(left, axis=1), taps, NT, preferred_element_type=jnp.float32
        )
        out_ref[comp] = total if add_ref is None else total + add_ref[comp, first_row:, :]


def lane_shift(low, high, shift):
    first, second = low[:, :LANE], low[:, LANE:]
    third, fourth = high[:, :LANE], high[:, LANE:]
    far = shift >= LANE
    parts = [
        jnp.where(far, second, first),
        jnp.where(far, third, second),
        jnp.where(far, fourth, third),
    ]
    step = shift & (LANE - 1)
    lane = lax.broadcasted_iota(jnp.int32, first.shape, 1)
    index = (lane + step) & (LANE - 1)
    turned = [jnp.take_along_axis(part, index, axis=1) for part in parts]
    stay = lane < LANE - step
    return jnp.concatenate(
        [jnp.where(stay, turned[0], turned[1]), jnp.where(stay, turned[1], turned[2])], axis=1
    )


def rows_kernel(
    tail_ref,
    taps_ref,
    near_ref,
    hot_ref,
    shift_ref,
    turn_ref,
    slots_ref,
    out_ref,
    win_ref,
    far_ref,
):
    me = lax.axis_index("pulse")
    half = (BLOCKS - SPANS + 1) * P_DEV
    win_ref[:ROWS, :] = jnp.zeros((ROWS, 3 * TILE), jnp.bfloat16)
    for n in range(SPANS - 1):
        rows = slice(ROWS + P_DEV * n, ROWS + P_DEV * n + P_DEV)
        real = tail_ref[0, :, TILE * n : TILE * n + TILE]
        win_ref[rows, :TILE] = real
        win_ref[rows, TILE : 2 * TILE] = tail_ref[1, :, TILE * n : TILE * n + TILE]
        win_ref[rows, 2 * TILE :] = -real
    correlate(win_ref, taps_ref, far_ref, half, 1, near_ref)
    series = jnp.concatenate(
        [
            jnp.concatenate([near_ref[0, :half, :], near_ref[1, :half, :]], axis=1),
            jnp.concatenate([far_ref[0], far_ref[1]], axis=1),
        ],
        axis=0,
    ).astype(jnp.bfloat16)
    picked = lax.dot_general(hot_ref[...], series, NN, preferred_element_type=jnp.float32)
    out_ref[...] = jnp.zeros_like(out_ref)
    for k in range(FOOT):
        rows = slice(P_DEV * k, P_DEV * k + P_DEV)
        low = picked[P_DEV * k : P_DEV * k + P_DEV]
        high = picked[P_DEV * (FOOT + k) : P_DEV * (FOOT + k) + P_DEV]
        shift = shift_ref[rows, :]
        real = lane_shift(low[:, :TILE], high[:, :TILE], shift)
        imag = lane_shift(low[:, TILE:], high[:, TILE:], shift)
        c = jnp.concatenate([turn_ref[0, rows, :]] * 2, axis=1)
        s = jnp.concatenate([turn_ref[1, rows, :]] * 2, axis=1)
        rot_real = ((real * c - imag * s) * FACTOR).astype(jnp.bfloat16)
        rot_imag = ((real * s + imag * c) * FACTOR).astype(jnp.bfloat16)
        slot = slots_ref[me, k]

        @pl.when(slot > 0)
        def _():
            owner = (slot - 1) >> 2
            out_ref[owner, 0] = rot_real
            out_ref[owner, 1] = rot_imag


def owner_kernel(local_ref, arrived_ref, steer_ref, image_ref, grad_ref, rows_ref, weight_ref):
    for d in range(N_PULSE):
        slot = local_ref[d, 0]
        for comp in range(2):
            piece = arrived_ref[d, comp]
            row = PULSES * comp + P_DEV * d
            for l in range(TILES_DEV):
                rows_ref[row : row + P_DEV, TILE * l : TILE * l + TILE] = jnp.where(
                    slot == l + 1, piece, jnp.zeros_like(piece)
                )
    for l in range(TILES_DEV):
        cols = slice(TILE * l, TILE * l + TILE)
        total = lax.dot_general(
            steer_ref[...], rows_ref[:, cols], NN, preferred_element_type=jnp.float32
        )
        image_ref[:, cols] = total
        real, imag = total[:TILE], total[TILE:]
        power = real * real + imag * imag
        weight_ref[:TILE, cols] = (-power * imag).astype(jnp.bfloat16)
        weight_ref[TILE:, cols] = (power * real).astype(jnp.bfloat16)
    sums = []
    for h in range(KDIM // TILE):
        cols = slice(TILE * h, TILE * h + TILE)
        back = lax.dot_general(
            weight_ref[...], rows_ref[cols, :], NT, preferred_element_type=jnp.float32
        )
        sums.append(
            jnp.sum(back * steer_ref[:, cols].astype(jnp.float32), axis=0, keepdims=True)
        )
    halves = [-4.0 * (sums[h] + sums[h + 2]) for h in range(2)]
    for c in range(PULSES // LANE):
        piece = halves[c // 2][:, LANE * (c % 2) : LANE * (c % 2) + LANE]
        for b in range(N_BAND):
            grad_ref[b, c : c + 1, :] = piece


def image_kernel(flat_ref, out_ref):
    for comp in range(2):
        out_ref[comp, 0] = flat_ref[TILE * comp : TILE * comp + TILE, :].T


def spread_kernel(bands_ref, out_ref):
    total = jnp.sum(bands_ref[...], axis=0)
    for m in range(N_PULSE):
        out_ref[m] = total


def final_kernel(parts_ref, out_ref):
    me = lax.axis_index("pulse")
    gradient = jnp.sum(parts_ref[...], axis=0)
    square = jnp.sum(jnp.sum(gradient * gradient, axis=0, keepdims=True), axis=1, keepdims=True)
    scaled = gradient / jnp.sqrt(square / PULSES + 1e-05)
    row = lax.broadcasted_iota(jnp.int32, scaled.shape, 0)
    own = jnp.sum(jnp.where(row == me >> 3, scaled, 0.0), axis=0, keepdims=True)
    turned = pltpu.roll(jnp.broadcast_to(own, (8, LANE)), (LANE - P_DEV * (me & 7)) & (LANE - 1), 1)
    out_ref[...] = turned[:1, :P_DEV]


def kernel(body, name, out_shape, scratch=(), cost=None, **extra):
    return pl.pallas_call(
        body,
        out_shape=out_shape,
        scratch_shapes=list(scratch),
        compiler_params=pltpu.CompilerParams(vmem_limit_bytes=VMEM_BYTES),
        cost_estimate=pl.CostEstimate(flops=0, bytes_accessed=cost, transcendentals=0) if cost else None,
        name=name,
        **extra,
    )


def on_device(echoes, replica, pulse_angles, footprint, tile_slot, offsets):
    bf16, f32, i32 = jnp.bfloat16, jnp.float32, jnp.int32
    shape = jax.ShapeDtypeStruct
    window = pltpu.VMEM((ROWS + P_DEV * (SPANS - 1), 3 * TILE), bf16)
    tail = lax.ppermute(echoes, "band", [(i, i - 1) for i in range(1, N_BAND)])
    taps = kernel(
        taps_kernel, "taps", shape((TILE, 2 * TILE * SPANS), bf16), cost=8 << 20
    )(replica)
    steer, slots, local, hot, shift, turn, near = kernel(
        prep_kernel,
        "prep",
        [
            shape((2 * TILE, KDIM), bf16),
            shape((N_PULSE, LANE), i32),
            shape((N_PULSE, LANE), i32),
            shape((ROWS, ROWS), bf16),
            shape((ROWS // 2, LANE), i32),
            shape((2, ROWS // 2, LANE), f32),
            shape((2, ROWS, TILE), f32),
        ],
        scratch=[window, pltpu.VMEM((LANE, FOOT), i32)],
        cost=12 << 20,
    )(taps, echoes, pulse_angles, footprint.T, tile_slot.reshape(1, NTILE), offsets.T)
    rows = kernel(
        rows_kernel,
        "rows",
        shape((N_PULSE, 2, P_DEV, TILE), bf16),
        scratch=[window, pltpu.VMEM((2, (SPANS - 1) * P_DEV, TILE), f32)],
    )(tail, taps, near, hot, shift, turn, slots)
    arrived = lax.all_to_all(rows, "pulse", split_axis=0, concat_axis=0, tiled=True)
    image_flat, grad = kernel(
        owner_kernel,
        "owner",
        [
            shape((2 * TILE, TILES_DEV * TILE), f32),
            shape((N_BAND, PULSES // LANE, LANE), f32),
        ],
        scratch=[
            pltpu.VMEM((KDIM, TILES_DEV * TILE), bf16),
            pltpu.VMEM((2 * TILE, TILES_DEV * TILE), bf16),
        ],
    )(local, arrived, steer)
    image = kernel(
        image_kernel,
        "image",
        shape((2, TILES_DEV, TILE, TILE), f32),
        grid=(TILES_DEV,),
        in_specs=[pl.BlockSpec((2 * TILE, TILE), lambda l: (0, l))],
        out_specs=pl.BlockSpec((2, 1, TILE, TILE), lambda l: (0, l, 0, 0)),
    )(image_flat)
    bands = lax.all_to_all(grad, "band", split_axis=0, concat_axis=0, tiled=True)
    spread = kernel(spread_kernel, "spread", shape((N_PULSE, PULSES // LANE, LANE), f32))(bands)
    parts = lax.all_to_all(spread, "pulse", split_axis=0, concat_axis=0, tiled=True)
    own = kernel(final_kernel, "final", shape((1, P_DEV), f32))(parts)
    return (image, own.reshape(P_DEV))


def solution(mesh):
    placed = (P(None, "pulse", "band"), P(), P(), P(), P(), P())
    return jax.shard_map(
        on_device,
        mesh=mesh,
        in_specs=placed,
        out_specs=(P(None, "pulse", "band", None), P("pulse")),
        check_vma=False,
    )
```

time: 72.4 us -> 67 us (0.925)
  blocking collectives: 10.9 us -> 37 us
  starting transfers between devices: 21.1 us -> 10 us
  waiting for transfers between devices: 16.4 us -> 6.93 us
  Pallas kernels: 16.4 us -> 11.1 us
  local copies, waits for them, and re-layouts: 5.06 us -> 0.73 us
    all_to_all x0 -> x1, blocking collectives: none -> 26.9 us  [on_device(): lax.all_to_all(rows, 'pulse', split_axis=0, concat_axis=0, tiled=True)]
    all_to_all x1 -> x0, starting transfers between devices: 11 us -> none  [on_device(): lax.all_to_all(rows, 'pulse', split_axis=0, concat_axis=0, tiled=True)]
    all_to_all x1 -> x0, waiting for transfers between devices: 9.77 us -> none  [on_device(): lax.all_to_all(rows, 'pulse', split_axis=0, concat_axis=0, tiled=True)]
    pallas_call x5 -> x7, Pallas kernels: 16.4 us -> 11.1 us  [the longest x1 2.53 us: on_device(): kernel(owner_kernel, 'owner', [shape((2 * TILE, TILES_DEV * TILE), f32),...]
    unnamed x16 -> x12, local copies, waits for them, and re-layouts: 3.84 us -> 0.73 us
    all_to_all x1, waiting for transfers between devices: 5.2 us -> 6.48 us  [on_device(): lax.all_to_all(spread, 'pulse', split_axis=0, concat_axis=0, tiled=True)]
    ppermute x1, waiting for transfers between devices: 1.39 us -> 0.46 us  [on_device(): tail = lax.ppermute(echoes, 'band', [(i, i - 1) for i in range(1, N_BAND)])]
    all_to_all x1, blocking collectives: 10.9 us -> 10.1 us  [on_device(): lax.all_to_all(grad, 'band', split_axis=0, concat_axis=0, tiled=True)]
  transfers between devices with their start and end apart: 3 -> 2, of which waited for: 3 -> 2; matrix products, arithmetic and copies ran while one was open for 1% -> 0% of each run, Pallas kernels for 12% -> 7%
where the time goes in v2:
time: 67 us; the launch traced here: 66.6 us
  blocking collectives  37 us (55%)
  Pallas kernels  11.1 us (17%)
  starting transfers between devices  10 us (15%)
  waiting for transfers between devices  6.93 us (10%)
  local copies, waits for them, and re-layouts  0.73 us (1%)
  between operations  0.73 us (1%)
    all_to_all x1, blocking collectives, on_device(): lax.all_to_all(rows, 'pulse', split_axis=0, concat_axis=0, tiled=True)  26.9 us
    all_to_all x1, blocking collectives, on_device(): lax.all_to_all(grad, 'band', split_axis=0, concat_axis=0, tiled=True)  10.1 us
    all_to_all x1, waiting for transfers between devices, on_device(): lax.all_to_all(spread, 'pulse', split_axis=0, concat_axis=0, tiled=True)  6.48 us
    ppermute x1, starting transfers between devices, on_device(): tail = lax.ppermute(echoes, 'band', [(i, i - 1) for i in range(1, N_BAND)])  5.28 us
    all_to_all x1, starting transfers between devices, on_device(): lax.all_to_all(spread, 'pulse', split_axis=0, concat_axis=0, tiled=True)  4.76 us
    pallas_call x1, Pallas kernels, on_device(): kernel(owner_kernel, 'owner', [shape((2 * TILE, TILES_DEV * TILE), f32),...  2.53 us
    pallas_call x1, Pallas kernels, on_device(): kernel(rows_kernel, 'rows', shape((N_PULSE, 2, P_DEV, TILE), bf16), scrat...  2.43 us
    pallas_call x1, Pallas kernels, on_device(): kernel(image_kernel, 'image', shape((2, TILES_DEV, TILE, TILE), f32), gri...  2.34 us
  transfers between devices with their start and end apart: 2, of which 2 were waited for; matrix products, arithmetic and copies ran while one was open for 0% of the time, Pallas kernels for 7%

profile of v2, /device:TPU:1, one launch (start us, length us, event | category | flops | bytes accessed | tf_op | source)
XLA Modules:
  0.0 66.6 jit_solution(9334846478610542845)
XLA Ops:
  0.6 0.0 copy-start
  0.6 0.0 copy-start.1
  0.7 5.3 %collective-permute-start = (bf16[2,16,4096]{2,1,0:T(8,128)(2,1)}, bf16[2,16,4096]{2,1,0:T(8,128)(2,1)S(1)}, u32[]{:S(2)}, u32[]{:S(2)}) collective-permute-start(bf16[2,16,4096]{2,1,0:T(8,128)(2,1)} %echo_ref.1), channel_id=1, source_target_pairs={{1,0},{2,1},{3,2},{4,3},{5,4},{6,5},{7,6},{9,8},{10,9},{11,10},{12... | collective-permute-start | bytes 786440 | tf_op jit(solution)/shard_map/ppermute | solution.py:307
  5.9 0.0 copy-start.2
  5.9 0.7 %copy-done.2 = bf16[2,2048]{1,0:T(2,128)(2,1)S(1)} copy-done((bf16[2,2048]{1,0:T(2,128)(2,1)S(1)}, bf16[2,2048]{1,0:T(2,128)(2,1)}, u32[]{:S(2)}) %copy-start.2) | copy-done | bytes 8216
  6.6 0.0 copy-start.3
  6.6 0.0 copy-start.4
  6.6 0.0 copy-start.5
  6.6 0.6 taps.1.taps_ref
  7.3 0.0 copy-done
  7.3 0.0 copy-done.1
  7.3 0.0 copy-done.3
  7.3 0.0 copy-done.4
  7.3 0.0 copy-done.5
  7.3 1.8 %prep.1 = (bf16[512,1024]{1,0:T(8,128)(2,1)S(1)}, s32[32,128]{1,0:T(8,128)S(1)}, s32[32,128]{1,0:T(8,128)S(1)}, bf16[256,256]{1,0:T(8,128)(2,1)S(1)}, s32[128,12...) custom-call(bf16[256,4608]{1,0:T(8,128)(2,1)S(1)} %taps.1.taps_ref, ...), custom_call_target="tpu_custom_call" | custom-call | bytes 12582912 | tf_op jit(solution)/shard_map/prep/pallas_call | solution.py:311
  9.2 0.5 collective-permute-done.tail_ref
  9.6 2.4 %rows.1 = bf16[32,2,16,256]{3,2,1,0:T(8,128)(2,1)S(1)} custom-call(bf16[2,16,4096]{2,1,0:T(8,128)(2,1)S(1)} %collective-permute-done.tail_ref, bf16[256,4608]{1,0:T(8,128)(2,1)S(1)} %taps.1.taps_ref, f32[2,256,256]{2,1,0:T(8,128)S(1)} %get-tuple-element.12.near_ref, bf16[256,256]{1,0:T(8,128)(2,1)S(1)} %get-tuple-element.13.hot_ref, ...), custom_call_target="tpu_custom_call" | custom-call | tf_op jit(solution)/shard_map/rows/pallas_call | solution.py:326
  12.1 26.9 %all_to_all.15.arrived_ref = bf16[32,2,16,256]{3,2,1,0:T(8,128)(2,1)S(1)} all-to-all(bf16[32,2,16,256]{3,2,1,0:T(8,128)(2,1)S(1)} %rows.1), channel_id=1, replica_groups=mesh['pulse'=32,'band'=8] {'pulse'}, dimensions={0} | all-to-all | bytes 1048576 | tf_op jit(solution)/shard_map/all_to_all | solution.py:332
  39.0 2.5 %owner.1 = (f32[512,1024]{1,0:T(8,128)S(1)}, f32[8,4,128]{2,1,0:T(4,128)S(1)}) custom-call(s32[32,128]{1,0:T(8,128)S(1)} %get-tuple-element.11.local_ref, bf16[32,2,16,256]{3,2,1,0:T(8,128)(2,1)S(1)} %all_to_all.15.arrived_ref, bf16[512,1024]{1,0:T(8,128)(2,1)S(1)} %get-tuple-element.17.steer_ref), custom_call_target="tpu_custom_call" | custom-call | tf_op jit(solution)/shard_map/owner/pallas_call | solution.py:333
  41.5 10.1 %all_to_all.16.bands_ref = f32[8,4,128]{2,1,0:T(4,128)S(1)} all-to-all(f32[8,4,128]{2,1,0:T(4,128)S(1)} %get-tuple-element.19), channel_id=1, replica_groups=mesh['pulse'=32,'band'=8] {'band'}, dimensions={0} | all-to-all | bytes 32768 | tf_op jit(solution)/shard_map/all_to_all | solution.py:353
  51.7 0.6 spread.1
  52.3 4.8 %all-to-all-start.2 = ((f32[32,4,128]{2,1,0:T(4,128)}), f32[32,4,128]{2,1,0:T(4,128)S(1)}, u32[]{:S(2)}, u32[]{:S(2)}) async-start(f32[32,4,128]{2,1,0:T(4,128)} %spread.1), calls=%async_computation.2 | async-start | bytes 131072 | tf_op jit(solution)/shard_map/all_to_all | solution.py:355
  57.1 2.3 %image.1 = f32[2,4,256,256]{3,2,1,0:T(8,128)} custom-call(f32[512,1024]{1,0:T(8,128)S(1)} %get-tuple-element.18.flat_ref), custom_call_target="tpu_custom_call" | custom-call | tf_op jit(solution)/shard_map/image/pallas_call | solution.py:345
  59.4 6.5 %all-to-all-done.2.parts_ref = f32[32,4,128]{2,1,0:T(4,128)S(1)} async-done(((f32[32,4,128]{2,1,0:T(4,128)}), f32[32,4,128]{2,1,0:T(4,128)S(1)}, u32[]{:S(2)}, u32[]{:S(2)}) %all-to-all-start.2) | async-done | bytes 65568 | tf_op jit(solution)/shard_map/all_to_all | solution.py:355
  65.9 0.7 %final.1 = f32[1,16]{1,0:T(1,128)} custom-call(f32[32,4,128]{2,1,0:T(4,128)S(1)} %all-to-all-done.2.parts_ref), custom_call_target="tpu_custom_call" | custom-call | tf_op jit(solution)/shard_map/final/pallas_call | solution.py:356
Async XLA Ops:
  0.6 6.7 %copy-start = (bf16[2,16,4096]{2,1,0:T(8,128)(2,1)S(1)}, bf16[2,16,4096]{2,1,0:T(8,128)(2,1)}, u32[]{:S(2)}) copy-start(bf16[2,16,4096]{2,1,0:T(8,128)(2,1)} %echo_ref.1) | copy-start | bytes 786436
  0.6 6.7 %copy-start.1 = (s32[512,8]{0,1:T(8,128)S(1)}, s32[512,8]{0,1:T(8,128)}, u32[]{:S(2)}) copy-start(s32[512,8]{0,1:T(8,128)} %param.11) | copy-start | bytes 49156
  0.7 9.0 %collective-permute-start = (bf16[2,16,4096]{2,1,0:T(8,128)(2,1)}, bf16[2,16,4096]{2,1,0:T(8,128)(2,1)S(1)}, u32[]{:S(2)}, u32[]{:S(2)}) collective-permute-start(bf16[2,16,4096]{2,1,0:T(8,128)(2,1)} %echo_ref.1), channel_id=1, source_target_pairs={{1,0},{2,1},{3,2},{4,3},{5,4},{6,5},{7,6},{9,8},{10,9},{11,10},{12... | collective-permute-start | bytes 786440 | tf_op jit(solution)/shard_map/ppermute | solution.py:307
  5.9 0.7 %copy-start.2 = (bf16[2,2048]{1,0:T(2,128)(2,1)S(1)}, bf16[2,2048]{1,0:T(2,128)(2,1)}, u32[]{:S(2)}) copy-start(bf16[2,2048]{1,0:T(2,128)(2,1)} %replica_ref.1) | copy-start | bytes 24580
  6.6 0.7 %copy-start.3 = (f32[3,512]{1,0:T(4,128)S(1)}, f32[3,512]{1,0:T(4,128)}, u32[]{:S(2)}) copy-start(f32[3,512]{1,0:T(4,128)} %angle_ref.1) | copy-start | bytes 18436
  6.6 0.7 %copy-start.4 = (s32[32,8]{0,1:T(8,128)S(1)}, s32[32,8]{0,1:T(8,128)}, u32[]{:S(2)}) copy-start(s32[32,8]{0,1:T(8,128)} %param.9) | copy-start | bytes 3076
  6.6 0.7 %copy-start.5 = (s32[128]{0:T(128)S(1)}, s32[128]{0:T(128)}, u32[]{:S(2)}) copy-start(s32[128]{0:T(128)} %param.10) | copy-start | bytes 1540
  52.3 13.6 %all-to-all-start.2 = ((f32[32,4,128]{2,1,0:T(4,128)}), f32[32,4,128]{2,1,0:T(4,128)S(1)}, u32[]{:S(2)}, u32[]{:S(2)}) async-start(f32[32,4,128]{2,1,0:T(4,128)} %spread.1), calls=%async_computation.2 | async-start | bytes 131072 | tf_op jit(solution)/shard_map/all_to_all | solution.py:355

commit v3 on v2

--- a/solution.py
+++ b/solution.py
@@ -34,15 +34,12 @@
 def taps_kernel(replica_ref, taps_ref):
     width = TAPS + LANE
     chunks = width // LANE
-    sub = lax.broadcasted_iota(jnp.int32, (8, width), 0)
     zero = jnp.zeros((16, LANE), jnp.bfloat16)
     for comp in range(2):
         line = replica_ref[comp : comp + 1, :].astype(jnp.float32)
         line = jnp.concatenate([line, jnp.zeros((1, LANE), jnp.float32)], axis=1)
         wide = jnp.broadcast_to(line, (8, width))
-        base = wide
-        for r in range(1, 8):
-            base = jnp.where(sub == r, pltpu.roll(wide, r, 1), base)
+        base = pltpu.roll(wide, 0, 1, stride=1, stride_axis=0)
         for j in range(8):
             first = base if j == 0 else pltpu.roll(base, 16 * j, 1)
             pair = jnp.concatenate([first, pltpu.roll(base, 16 * j + 8, 1)], axis=0)
@@ -147,17 +144,23 @@
 
 def correlate(win_ref, taps_ref, out_ref, first_row, first_span, add_ref):
     count = out_ref.shape[1]
-    spans = range(first_span, SPANS)
-    taps = taps_ref[:, 512 * first_span :]
+    left = []
     for comp in range(2):
         cols = slice(TILE * comp, TILE * comp + 2 * TILE)
-        left = [
-            win_ref[first_row + P_DEV * a : first_row + P_DEV * a + count, cols] for a in spans
+        spans = [
+            win_ref[first_row + P_DEV * a : first_row + P_DEV * a + count, cols]
+            for a in range(first_span, SPANS)
         ]
-        total = lax.dot_general(
-            jnp.concatenate(left, axis=1), taps, NT, preferred_element_type=jnp.float32
-        )
-        out_ref[comp] = total if add_ref is None else total + add_ref[comp, first_row:, :]
+        left.append(jnp.concatenate(spans, axis=1))
+    total = lax.dot_general(
+        jnp.concatenate(left, axis=0),
+        taps_ref[:, 2 * TILE * first_span :],
+        NT,
+        preferred_element_type=jnp.float32,
+    )
+    for comp in range(2):
+        part = total[count * comp : count * comp + count]
+        out_ref[comp] = part if add_ref is None else part + add_ref[comp, first_row:, :]
 
 
 def lane_shift(low, high, shift):
@@ -210,7 +213,7 @@
     ).astype(jnp.bfloat16)
     picked = lax.dot_general(hot_ref[...], series, NN, preferred_element_type=jnp.float32)
     out_ref[...] = jnp.zeros_like(out_ref)
-    for k in range(FOOT):
+    for k in reversed(range(FOOT)):
         rows = slice(P_DEV * k, P_DEV * k + P_DEV)
         low = picked[P_DEV * k : P_DEV * k + P_DEV]
         high = picked[P_DEV * (FOOT + k) : P_DEV * (FOOT + k) + P_DEV]
@@ -219,15 +222,10 @@
         imag = lane_shift(low[:, TILE:], high[:, TILE:], shift)
         c = jnp.concatenate([turn_ref[0, rows, :]] * 2, axis=1)
         s = jnp.concatenate([turn_ref[1, rows, :]] * 2, axis=1)
-        rot_real = ((real * c - imag * s) * FACTOR).astype(jnp.bfloat16)
-        rot_imag = ((real * s + imag * c) * FACTOR).astype(jnp.bfloat16)
         slot = slots_ref[me, k]
-
-        @pl.when(slot > 0)
-        def _():
-            owner = (slot - 1) >> 2
-            out_ref[owner, 0] = rot_real
-            out_ref[owner, 1] = rot_imag
+        owner = (jnp.where(slot > 0, slot, slots_ref[me, 0]) - 1) >> 2
+        out_ref[owner, 0] = ((real * c - imag * s) * FACTOR).astype(jnp.bfloat16)
+        out_ref[owner, 1] = ((real * s + imag * c) * FACTOR).astype(jnp.bfloat16)
 
 
 def owner_kernel(local_ref, arrived_ref, steer_ref, image_ref, grad_ref, rows_ref, weight_ref):

time: 67 us -> 65.8 us (0.982)
  Pallas kernels: 11.1 us -> 9.76 us
    pallas_call x1, Pallas kernels: 2.43 us -> 1.21 us  [on_device(): kernel(rows_kernel, 'rows', shape((N_PULSE, 2, P_DEV, TILE), bf16), scrat...]
where the time goes in v3:
time: 65.8 us; the launch traced here: 65.4 us
  blocking collectives  37 us (56%)
  starting transfers between devices  10 us (15%)
  Pallas kernels  9.76 us (15%)
  waiting for transfers between devices  6.96 us (11%)
  local copies, waits for them, and re-layouts  0.86 us (1%)
  between operations  0.73 us (1%)
    all_to_all x1, blocking collectives, on_device(): lax.all_to_all(rows, 'pulse', split_axis=0, concat_axis=0, tiled=True)  26.9 us
    all_to_all x1, blocking collectives, on_device(): lax.all_to_all(grad, 'band', split_axis=0, concat_axis=0, tiled=True)  10.2 us
    all_to_all x1, waiting for transfers between devices, on_device(): lax.all_to_all(spread, 'pulse', split_axis=0, concat_axis=0, tiled=True)  6.48 us
    ppermute x1, starting transfers between devices, on_device(): tail = lax.ppermute(echoes, 'band', [(i, i - 1) for i in range(1, N_BAND)])  5.28 us
    all_to_all x1, starting transfers between devices, on_device(): lax.all_to_all(spread, 'pulse', split_axis=0, concat_axis=0, tiled=True)  4.76 us
    pallas_call x1, Pallas kernels, on_device(): kernel(owner_kernel, 'owner', [shape((2 * TILE, TILES_DEV * TILE), f32),...  2.53 us
    pallas_call x1, Pallas kernels, on_device(): kernel(image_kernel, 'image', shape((2, TILES_DEV, TILE, TILE), f32), gri...  2.34 us
    pallas_call x1, Pallas kernels, on_device(): kernel(prep_kernel, 'prep', [shape((2 * TILE, KDIM), bf16), shape((N_PULS...  1.8 us
  transfers between devices with their start and end apart: 2, of which 2 were waited for; matrix products, arithmetic and copies ran while one was open for 0% of the time, Pallas kernels for 7%

profile of v3, /device:TPU:1, one launch (start us, length us, event | category | flops | bytes accessed | tf_op | source)
XLA Modules:
  0.0 65.4 jit_solution(6067118879946912909)
XLA Ops:
  0.6 0.0 copy-start
  0.6 0.0 copy-start.1
  0.7 5.3 %collective-permute-start = (bf16[2,16,4096]{2,1,0:T(8,128)(2,1)}, bf16[2,16,4096]{2,1,0:T(8,128)(2,1)S(1)}, u32[]{:S(2)}, u32[]{:S(2)}) collective-permute-start(bf16[2,16,4096]{2,1,0:T(8,128)(2,1)} %echo_ref.1), channel_id=1, source_target_pairs={{1,0},{2,1},{3,2},{4,3},{5,4},{6,5},{7,6},{9,8},{10,9},{11,10},{12... | collective-permute-start | bytes 786440 | tf_op jit(solution)/shard_map/ppermute | solution.py:305
  5.9 0.0 copy-start.2
  5.9 0.7 %copy-done.2 = bf16[2,2048]{1,0:T(2,128)(2,1)S(1)} copy-done((bf16[2,2048]{1,0:T(2,128)(2,1)S(1)}, bf16[2,2048]{1,0:T(2,128)(2,1)}, u32[]{:S(2)}) %copy-start.2) | copy-done | bytes 8216
  6.6 0.0 copy-start.3
  6.6 0.0 copy-start.4
  6.6 0.0 copy-start.5
  6.6 0.5 taps.1.taps_ref
  7.2 0.0 copy-done
  7.2 0.0 copy-done.1
  7.2 0.1 copy-done.3
  7.3 0.0 copy-done.4
  7.3 0.0 copy-done.5
  7.3 1.8 %prep.1 = (bf16[512,1024]{1,0:T(8,128)(2,1)S(1)}, s32[32,128]{1,0:T(8,128)S(1)}, s32[32,128]{1,0:T(8,128)S(1)}, bf16[256,256]{1,0:T(8,128)(2,1)S(1)}, s32[128,12...) custom-call(bf16[256,4608]{1,0:T(8,128)(2,1)S(1)} %taps.1.taps_ref, ...), custom_call_target="tpu_custom_call" | custom-call | bytes 12582912 | tf_op jit(solution)/shard_map/prep/pallas_call | solution.py:309
  9.2 0.5 collective-permute-done.tail_ref
  9.6 1.2 %rows.1 = bf16[32,2,16,256]{3,2,1,0:T(8,128)(2,1)S(1)} custom-call(bf16[2,16,4096]{2,1,0:T(8,128)(2,1)S(1)} %collective-permute-done.tail_ref, bf16[256,4608]{1,0:T(8,128)(2,1)S(1)} %taps.1.taps_ref, f32[2,256,256]{2,1,0:T(8,128)S(1)} %get-tuple-element.12.near_ref, bf16[256,256]{1,0:T(8,128)(2,1)S(1)} %get-tuple-element.13.hot_ref, ...), custom_call_target="tpu_custom_call" | custom-call | tf_op jit(solution)/shard_map/rows/pallas_call | solution.py:324
  10.9 26.9 %all_to_all.15.arrived_ref = bf16[32,2,16,256]{3,2,1,0:T(8,128)(2,1)S(1)} all-to-all(bf16[32,2,16,256]{3,2,1,0:T(8,128)(2,1)S(1)} %rows.1), channel_id=1, replica_groups=mesh['pulse'=32,'band'=8] {'pulse'}, dimensions={0} | all-to-all | bytes 1048576 | tf_op jit(solution)/shard_map/all_to_all | solution.py:330
  37.7 2.5 %owner.1 = (f32[512,1024]{1,0:T(8,128)S(1)}, f32[8,4,128]{2,1,0:T(4,128)S(1)}) custom-call(s32[32,128]{1,0:T(8,128)S(1)} %get-tuple-element.11.local_ref, bf16[32,2,16,256]{3,2,1,0:T(8,128)(2,1)S(1)} %all_to_all.15.arrived_ref, bf16[512,1024]{1,0:T(8,128)(2,1)S(1)} %get-tuple-element.17.steer_ref), custom_call_target="tpu_custom_call" | custom-call | tf_op jit(solution)/shard_map/owner/pallas_call | solution.py:331
  40.3 10.2 %all_to_all.16.bands_ref = f32[8,4,128]{2,1,0:T(4,128)S(1)} all-to-all(f32[8,4,128]{2,1,0:T(4,128)S(1)} %get-tuple-element.19), channel_id=1, replica_groups=mesh['pulse'=32,'band'=8] {'band'}, dimensions={0} | all-to-all | bytes 32768 | tf_op jit(solution)/shard_map/all_to_all | solution.py:351
  50.4 0.6 spread.1
  51.1 4.8 %all-to-all-start.2 = ((f32[32,4,128]{2,1,0:T(4,128)}), f32[32,4,128]{2,1,0:T(4,128)S(1)}, u32[]{:S(2)}, u32[]{:S(2)}) async-start(f32[32,4,128]{2,1,0:T(4,128)} %spread.1), calls=%async_computation.2 | async-start | bytes 131072 | tf_op jit(solution)/shard_map/all_to_all | solution.py:353
  55.9 2.3 %image.1 = f32[2,4,256,256]{3,2,1,0:T(8,128)} custom-call(f32[512,1024]{1,0:T(8,128)S(1)} %get-tuple-element.18.flat_ref), custom_call_target="tpu_custom_call" | custom-call | tf_op jit(solution)/shard_map/image/pallas_call | solution.py:343
  58.2 6.5 %all-to-all-done.2.parts_ref = f32[32,4,128]{2,1,0:T(4,128)S(1)} async-done(((f32[32,4,128]{2,1,0:T(4,128)}), f32[32,4,128]{2,1,0:T(4,128)S(1)}, u32[]{:S(2)}, u32[]{:S(2)}) %all-to-all-start.2) | async-done | bytes 65568 | tf_op jit(solution)/shard_map/all_to_all | solution.py:353
  64.7 0.7 %final.1 = f32[1,16]{1,0:T(1,128)} custom-call(f32[32,4,128]{2,1,0:T(4,128)S(1)} %all-to-all-done.2.parts_ref), custom_call_target="tpu_custom_call" | custom-call | tf_op jit(solution)/shard_map/final/pallas_call | solution.py:354
Async XLA Ops:
  0.6 6.5 %copy-start = (bf16[2,16,4096]{2,1,0:T(8,128)(2,1)S(1)}, bf16[2,16,4096]{2,1,0:T(8,128)(2,1)}, u32[]{:S(2)}) copy-start(bf16[2,16,4096]{2,1,0:T(8,128)(2,1)} %echo_ref.1) | copy-start | bytes 786436
  0.6 6.5 %copy-start.1 = (s32[512,8]{0,1:T(8,128)S(1)}, s32[512,8]{0,1:T(8,128)}, u32[]{:S(2)}) copy-start(s32[512,8]{0,1:T(8,128)} %param.11) | copy-start | bytes 49156
  0.7 9.0 %collective-permute-start = (bf16[2,16,4096]{2,1,0:T(8,128)(2,1)}, bf16[2,16,4096]{2,1,0:T(8,128)(2,1)S(1)}, u32[]{:S(2)}, u32[]{:S(2)}) collective-permute-start(bf16[2,16,4096]{2,1,0:T(8,128)(2,1)} %echo_ref.1), channel_id=1, source_target_pairs={{1,0},{2,1},{3,2},{4,3},{5,4},{6,5},{7,6},{9,8},{10,9},{11,10},{12... | collective-permute-start | bytes 786440 | tf_op jit(solution)/shard_map/ppermute | solution.py:305
  5.9 0.7 %copy-start.2 = (bf16[2,2048]{1,0:T(2,128)(2,1)S(1)}, bf16[2,2048]{1,0:T(2,128)(2,1)}, u32[]{:S(2)}) copy-start(bf16[2,2048]{1,0:T(2,128)(2,1)} %replica_ref.1) | copy-start | bytes 24580
  6.6 0.7 %copy-start.3 = (f32[3,512]{1,0:T(4,128)S(1)}, f32[3,512]{1,0:T(4,128)}, u32[]{:S(2)}) copy-start(f32[3,512]{1,0:T(4,128)} %angle_ref.1) | copy-start | bytes 18436
  6.6 0.7 %copy-start.4 = (s32[32,8]{0,1:T(8,128)S(1)}, s32[32,8]{0,1:T(8,128)}, u32[]{:S(2)}) copy-start(s32[32,8]{0,1:T(8,128)} %param.9) | copy-start | bytes 3076
  6.6 0.7 %copy-start.5 = (s32[128]{0:T(128)S(1)}, s32[128]{0:T(128)}, u32[]{:S(2)}) copy-start(s32[128]{0:T(128)} %param.10) | copy-start | bytes 1540
  51.1 13.6 %all-to-all-start.2 = ((f32[32,4,128]{2,1,0:T(4,128)}), f32[32,4,128]{2,1,0:T(4,128)S(1)}, u32[]{:S(2)}, u32[]{:S(2)}) async-start(f32[32,4,128]{2,1,0:T(4,128)} %spread.1), calls=%async_computation.2 | async-start | bytes 131072 | tf_op jit(solution)/shard_map/all_to_all | solution.py:353

commit v4 on v3

--- a/solution.py
+++ b/solution.py
@@ -228,7 +228,18 @@
         out_ref[owner, 1] = ((real * s + imag * c) * FACTOR).astype(jnp.bfloat16)
 
 
-def owner_kernel(local_ref, arrived_ref, steer_ref, image_ref, grad_ref, rows_ref, weight_ref):
+def owner_kernel(
+    local_ref,
+    arrived_ref,
+    steer_ref,
+    image_hbm,
+    grad_ref,
+    rows_ref,
+    weight_ref,
+    flat_ref,
+    image_ref,
+    image_sem,
+):
     for d in range(N_PULSE):
         slot = local_ref[d, 0]
         for comp in range(2):
@@ -238,46 +249,54 @@
                 rows_ref[row : row + P_DEV, TILE * l : TILE * l + TILE] = jnp.where(
                     slot == l + 1, piece, jnp.zeros_like(piece)
                 )
+    copies, sums = [], []
+
+    def write_out(l):
+        cols = slice(TILE * l, TILE * l + TILE)
+        for c in range(2):
+            image_ref[l, c] = flat_ref[TILE * c : TILE * c + TILE, cols].T
+            copy = pltpu.make_async_copy(image_ref.at[l, c], image_hbm.at[c, l], image_sem.at[l, c])
+            copy.start()
+            copies.append(copy)
+
     for l in range(TILES_DEV):
         cols = slice(TILE * l, TILE * l + TILE)
         total = lax.dot_general(
             steer_ref[...], rows_ref[:, cols], NN, preferred_element_type=jnp.float32
         )
-        image_ref[:, cols] = total
+        flat_ref[:, cols] = total
+        if l > 0:
+            write_out(l - 1)
         real, imag = total[:TILE], total[TILE:]
         power = real * real + imag * imag
         weight_ref[:TILE, cols] = (-power * imag).astype(jnp.bfloat16)
         weight_ref[TILE:, cols] = (power * real).astype(jnp.bfloat16)
-    sums = []
     for h in range(KDIM // TILE):
         cols = slice(TILE * h, TILE * h + TILE)
         back = lax.dot_general(
             weight_ref[...], rows_ref[cols, :], NT, preferred_element_type=jnp.float32
         )
+        if h == 0:
+            write_out(TILES_DEV - 1)
         sums.append(
             jnp.sum(back * steer_ref[:, cols].astype(jnp.float32), axis=0, keepdims=True)
         )
     halves = [-4.0 * (sums[h] + sums[h + 2]) for h in range(2)]
     for c in range(PULSES // LANE):
-        piece = halves[c // 2][:, LANE * (c % 2) : LANE * (c % 2) + LANE]
-        for b in range(N_BAND):
-            grad_ref[b, c : c + 1, :] = piece
-
-
-def image_kernel(flat_ref, out_ref):
-    for comp in range(2):
-        out_ref[comp, 0] = flat_ref[TILE * comp : TILE * comp + TILE, :].T
-
-
-def spread_kernel(bands_ref, out_ref):
-    total = jnp.sum(bands_ref[...], axis=0)
-    for m in range(N_PULSE):
+        grad_ref[c : c + 1, :] = halves[c // 2][:, LANE * (c % 2) : LANE * (c % 2) + LANE]
+    for copy in copies:
+        copy.wait()
+
+
+def spread_kernel(own_ref, other_ref, out_ref):
+    total = (own_ref[...] + other_ref[...]).astype(jnp.bfloat16)
+    for m in range(N_PULSE * N_BAND // 2):
         out_ref[m] = total
 
 
 def final_kernel(parts_ref, out_ref):
     me = lax.axis_index("pulse")
-    gradient = jnp.sum(parts_ref[...], axis=0)
+    gradient = jnp.sum(parts_ref[...].astype(jnp.float32), axis=0)
     square = jnp.sum(jnp.sum(gradient * gradient, axis=0, keepdims=True), axis=1, keepdims=True)
     scaled = gradient / jnp.sqrt(square / PULSES + 1e-05)
     row = lax.broadcasted_iota(jnp.int32, scaled.shape, 0)
@@ -328,29 +347,35 @@
         scratch=[window, pltpu.VMEM((2, (SPANS - 1) * P_DEV, TILE), f32)],
     )(tail, taps, near, hot, shift, turn, slots)
     arrived = lax.all_to_all(rows, "pulse", split_axis=0, concat_axis=0, tiled=True)
-    image_flat, grad = kernel(
+    image, grad = kernel(
         owner_kernel,
         "owner",
         [
-            shape((2 * TILE, TILES_DEV * TILE), f32),
-            shape((N_BAND, PULSES // LANE, LANE), f32),
+            shape((2, TILES_DEV, TILE, TILE), f32),
+            shape((PULSES // LANE, LANE), f32),
         ],
+        out_specs=[pl.BlockSpec(memory_space=pl.ANY), pl.BlockSpec(memory_space=pltpu.VMEM)],
         scratch=[
             pltpu.VMEM((KDIM, TILES_DEV * TILE), bf16),
             pltpu.VMEM((2 * TILE, TILES_DEV * TILE), bf16),
+            pltpu.VMEM((2 * TILE, TILES_DEV * TILE), f32),
+            pltpu.VMEM((TILES_DEV, 2, TILE, TILE), f32),
+            pltpu.SemaphoreType.DMA((TILES_DEV, 2)),
         ],
     )(local, arrived, steer)
-    image = kernel(
-        image_kernel,
-        "image",
-        shape((2, TILES_DEV, TILE, TILE), f32),
-        grid=(TILES_DEV,),
-        in_specs=[pl.BlockSpec((2 * TILE, TILE), lambda l: (0, l))],
-        out_specs=pl.BlockSpec((2, 1, TILE, TILE), lambda l: (0, l, 0, 0)),
-    )(image_flat)
-    bands = lax.all_to_all(grad, "band", split_axis=0, concat_axis=0, tiled=True)
-    spread = kernel(spread_kernel, "spread", shape((N_PULSE, PULSES // LANE, LANE), f32))(bands)
-    parts = lax.all_to_all(spread, "pulse", split_axis=0, concat_axis=0, tiled=True)
+    other = lax.ppermute(grad, "band", [(i, i ^ 1) for i in range(N_BAND)])
+    chips = N_PULSE * N_BAND // 2
+    spread = kernel(spread_kernel, "spread", shape((chips, PULSES // LANE, LANE), bf16))(
+        grad, other
+    )
+    parts = lax.all_to_all(
+        spread,
+        ("pulse", "band"),
+        split_axis=0,
+        concat_axis=0,
+        axis_index_groups=[list(range(core, 2 * chips, 2)) for core in range(2)],
+        tiled=True,
+    )
     own = kernel(final_kernel, "final", shape((1, P_DEV), f32))(parts)
     return (image, own.reshape(P_DEV))
 

time: 65.8 us -> 65 us (0.988)
  blocking collectives: 37 us -> 48.4 us
  waiting for transfers between devices: 6.96 us -> 1.62 us
  starting transfers between devices: 10 us -> 5.37 us
  Pallas kernels: 9.76 us -> 7.7 us
    all_to_all x1, blocking collectives: 10.2 us -> 21.5 us  [on_device(): lax.all_to_all(spread, ('pulse', 'band'), split_axis=0, concat_axis=0, ax...]
    all_to_all x1 -> x0, waiting for transfers between devices: 6.48 us -> none  [on_device(): lax.all_to_all(spread, 'pulse', split_axis=0, concat_axis=0, tiled=True)]
    all_to_all x1 -> x0, starting transfers between devices: 4.76 us -> none  [on_device(): lax.all_to_all(spread, 'pulse', split_axis=0, concat_axis=0, tiled=True)]
    pallas_call x3 -> x2, Pallas kernels: 5.52 us -> 3.35 us  [the longest x1 3.32 us: on_device(): kernel(owner_kernel, 'owner', [shape((2, TILES_DEV, TILE, TILE), f32), sh...]
    ppermute x0 -> x1, waiting for transfers between devices: none -> 1.14 us  [on_device(): other = lax.ppermute(grad, 'band', [(i, i ^ 1) for i in range(N_BAND)])]
  transfers between devices with their start and end apart: 2 -> 2, of which waited for: 2 -> 2; matrix products, arithmetic and copies ran while one was open for 0% -> 0% of each run, Pallas kernels for 7% -> 4%
where the time goes in v4:
time: 65 us; the launch traced here: 64.7 us
  blocking collectives  48.4 us (74%)
  Pallas kernels  7.7 us (12%)
  starting transfers between devices  5.37 us (8%)
  waiting for transfers between devices  1.62 us (2%)
  local copies, waits for them, and re-layouts  0.86 us (1%)
  between operations  0.73 us (1%)
    all_to_all x1, blocking collectives, on_device(): lax.all_to_all(rows, 'pulse', split_axis=0, concat_axis=0, tiled=True)  26.9 us
    all_to_all x1, blocking collectives, on_device(): lax.all_to_all(spread, ('pulse', 'band'), split_axis=0, concat_axis=0, ax...  21.5 us
    ppermute x1, starting transfers between devices, on_device(): tail = lax.ppermute(echoes, 'band', [(i, i - 1) for i in range(1, N_BAND)])  5.28 us
    pallas_call x1, Pallas kernels, on_device(): kernel(owner_kernel, 'owner', [shape((2, TILES_DEV, TILE, TILE), f32), sh...  3.32 us
    pallas_call x1, Pallas kernels, on_device(): kernel(prep_kernel, 'prep', [shape((2 * TILE, KDIM), bf16), shape((N_PULS...  1.8 us
  transfers between devices with their start and end apart: 2, of which 2 were waited for; matrix products, arithmetic and copies ran while one was open for 0% of the time, Pallas kernels for 4%

profile of v4, /device:TPU:1, one launch (start us, length us, event | category | flops | bytes accessed | tf_op | source)
XLA Modules:
  0.0 64.7 jit_solution(3861698829664452451)
XLA Ops:
  0.6 0.0 copy-start
  0.6 0.0 copy-start.1
  0.7 5.3 %collective-permute-start = (bf16[2,16,4096]{2,1,0:T(8,128)(2,1)}, bf16[2,16,4096]{2,1,0:T(8,128)(2,1)S(1)}, u32[]{:S(2)}, u32[]{:S(2)}) collective-permute-start(bf16[2,16,4096]{2,1,0:T(8,128)(2,1)} %echo_ref.1), channel_id=1, source_target_pairs={{1,0},{2,1},{3,2},{4,3},{5,4},{6,5},{7,6},{9,8},{10,9},{11,10},{12... | collective-permute-start | bytes 786440 | tf_op jit(solution)/shard_map/ppermute | solution.py:324
  5.9 0.0 copy-start.2
  5.9 0.7 %copy-done.2 = bf16[2,2048]{1,0:T(2,128)(2,1)S(1)} copy-done((bf16[2,2048]{1,0:T(2,128)(2,1)S(1)}, bf16[2,2048]{1,0:T(2,128)(2,1)}, u32[]{:S(2)}) %copy-start.2) | copy-done | bytes 8216
  6.6 0.0 copy-start.3
  6.6 0.0 copy-start.4
  6.6 0.0 copy-start.5
  6.6 0.5 taps.1.taps_ref
  7.2 0.0 copy-done
  7.2 0.0 copy-done.1
  7.2 0.1 copy-done.3
  7.3 0.0 copy-done.4
  7.3 0.0 copy-done.5
  7.3 1.8 %prep.1 = (bf16[512,1024]{1,0:T(8,128)(2,1)S(1)}, s32[32,128]{1,0:T(8,128)S(1)}, s32[32,128]{1,0:T(8,128)S(1)}, bf16[256,256]{1,0:T(8,128)(2,1)S(1)}, s32[128,12...) custom-call(bf16[256,4608]{1,0:T(8,128)(2,1)S(1)} %taps.1.taps_ref, ...), custom_call_target="tpu_custom_call" | custom-call | bytes 12582912 | tf_op jit(solution)/shard_map/prep/pallas_call | solution.py:328
  9.2 0.5 collective-permute-done.tail_ref
  9.6 1.2 %rows.1 = bf16[32,2,16,256]{3,2,1,0:T(8,128)(2,1)S(1)} custom-call(bf16[2,16,4096]{2,1,0:T(8,128)(2,1)S(1)} %collective-permute-done.tail_ref, bf16[256,4608]{1,0:T(8,128)(2,1)S(1)} %taps.1.taps_ref, f32[2,256,256]{2,1,0:T(8,128)S(1)} %get-tuple-element.12.near_ref, bf16[256,256]{1,0:T(8,128)(2,1)S(1)} %get-tuple-element.13.hot_ref, ...), custom_call_target="tpu_custom_call" | custom-call | tf_op jit(solution)/shard_map/rows/pallas_call | solution.py:343
  10.9 26.9 %all_to_all.10.arrived_ref = bf16[32,2,16,256]{3,2,1,0:T(8,128)(2,1)S(1)} all-to-all(bf16[32,2,16,256]{3,2,1,0:T(8,128)(2,1)S(1)} %rows.1), channel_id=1, replica_groups=mesh['pulse'=32,'band'=8] {'pulse'}, dimensions={0} | all-to-all | bytes 1048576 | tf_op jit(solution)/shard_map/all_to_all | solution.py:349
  37.7 3.3 %owner.1 = (f32[2,4,256,256]{3,2,1,0:T(8,128)}, f32[4,128]{1,0:T(4,128)S(1)}) custom-call(s32[32,128]{1,0:T(8,128)S(1)} %get-tuple-element.11.local_ref, bf16[32,2,16,256]{3,2,1,0:T(8,128)(2,1)S(1)} %all_to_all.10.arrived_ref, bf16[512,1024]{1,0:T(8,128)(2,1)S(1)} %get-tuple-element.17.steer_ref), custom_call_target="tpu_custom_call" | custom-call | tf_op jit(solution)/shard_map/owner/pallas_call | solution.py:350
  41.1 0.1 collective-permute-start.1
  41.2 1.1 %collective-permute-done.1.other_ref = f32[4,128]{1,0:T(4,128)S(1)} collective-permute-done((f32[4,128]{1,0:T(4,128)S(1)}, f32[4,128]{1,0:T(4,128)S(1)}, u32[]{:S(2)}, u32[]{:S(2)}) %collective-permute-start.1) | collective-permute-done | bytes 2080 | tf_op jit(solution)/shard_map/ppermute | solution.py:366
  42.3 21.5 %all_to_all.11.parts_ref = bf16[128,4,128]{2,1,0:T(4,128)(2,1)S(1)} all-to-all(bf16[128,4,128]{2,1,0:T(4,128)(2,1)S(1)} %spread.1), channel_id=1, replica_groups={{0,2,4,6,8,10,12,14,16,18,20,22,24,26,28,30,32,34,36,38,40,42,44,46,48,..., dimensions={0} | all-to-all | bytes 262144 | tf_op jit(solution)/shard_map/all_to_all | solution.py:371
  63.9 0.8 %final.1 = f32[1,16]{1,0:T(1,128)} custom-call(bf16[128,4,128]{2,1,0:T(4,128)(2,1)S(1)} %all_to_all.11.parts_ref), custom_call_target="tpu_custom_call" | custom-call | tf_op jit(solution)/shard_map/final/pallas_call | solution.py:379
  (1 shorter events, 0.0 us)
Async XLA Ops:
  0.6 6.5 %copy-start = (bf16[2,16,4096]{2,1,0:T(8,128)(2,1)S(1)}, bf16[2,16,4096]{2,1,0:T(8,128)(2,1)}, u32[]{:S(2)}) copy-start(bf16[2,16,4096]{2,1,0:T(8,128)(2,1)} %echo_ref.1) | copy-start | bytes 786436
  0.6 6.5 %copy-start.1 = (s32[512,8]{0,1:T(8,128)S(1)}, s32[512,8]{0,1:T(8,128)}, u32[]{:S(2)}) copy-start(s32[512,8]{0,1:T(8,128)} %param.11) | copy-start | bytes 49156
  0.7 9.0 %collective-permute-start = (bf16[2,16,4096]{2,1,0:T(8,128)(2,1)}, bf16[2,16,4096]{2,1,0:T(8,128)(2,1)S(1)}, u32[]{:S(2)}, u32[]{:S(2)}) collective-permute-start(bf16[2,16,4096]{2,1,0:T(8,128)(2,1)} %echo_ref.1), channel_id=1, source_target_pairs={{1,0},{2,1},{3,2},{4,3},{5,4},{6,5},{7,6},{9,8},{10,9},{11,10},{12... | collective-permute-start | bytes 786440 | tf_op jit(solution)/shard_map/ppermute | solution.py:324
  5.9 0.7 %copy-start.2 = (bf16[2,2048]{1,0:T(2,128)(2,1)S(1)}, bf16[2,2048]{1,0:T(2,128)(2,1)}, u32[]{:S(2)}) copy-start(bf16[2,2048]{1,0:T(2,128)(2,1)} %replica_ref.1) | copy-start | bytes 24580
  6.6 0.7 %copy-start.3 = (f32[3,512]{1,0:T(4,128)S(1)}, f32[3,512]{1,0:T(4,128)}, u32[]{:S(2)}) copy-start(f32[3,512]{1,0:T(4,128)} %angle_ref.1) | copy-start | bytes 18436
  6.6 0.7 %copy-start.4 = (s32[32,8]{0,1:T(8,128)S(1)}, s32[32,8]{0,1:T(8,128)}, u32[]{:S(2)}) copy-start(s32[32,8]{0,1:T(8,128)} %param.9) | copy-start | bytes 3076
  6.6 0.7 %copy-start.5 = (s32[128]{0:T(128)S(1)}, s32[128]{0:T(128)}, u32[]{:S(2)}) copy-start(s32[128]{0:T(128)} %param.10) | copy-start | bytes 1540
  41.1 1.2 %collective-permute-start.1 = (f32[4,128]{1,0:T(4,128)S(1)}, f32[4,128]{1,0:T(4,128)S(1)}, u32[]{:S(2)}, u32[]{:S(2)}) collective-permute-start(f32[4,128]{1,0:T(4,128)S(1)} %get-tuple-element.19.own_ref), channel_id=1, source_target_pairs={{0,1},{1,0},{2,3},{3,2},{4,5},{5,4},{6,7},{7,6},{8,9},{9,8},{10,11... | collective-permute-start | bytes 6152 | tf_op jit(solution)/shard_map/ppermute | solution.py:366

commit v5 on v4

--- a/solution.py
+++ b/solution.py
@@ -108,12 +108,13 @@
     listed = jnp.concatenate([footprint_ref[...], jnp.full((FOOT, LANE - N_PULSE), -1)], axis=1)
     listed = listed.T
     listed_ref[...] = listed
+    places = (slot_ref[...] + 1).astype(jnp.float32)
     lane = lax.broadcasted_iota(jnp.int32, (N_PULSE, LANE), 1)
     slots = jnp.zeros((N_PULSE, LANE), jnp.int32)
     local = jnp.zeros((N_PULSE, 1), jnp.int32)
     for k in range(FOOT):
         same = listed[:N_PULSE, k : k + 1] == lane
-        slot = jnp.sum(jnp.where(same, slot_ref[...] + 1, 0), axis=1, keepdims=True)
+        slot = jnp.sum(jnp.where(same, places, 0.0), axis=1, keepdims=True).astype(jnp.int32)
         slots = jnp.where(lane == k, slot, slots)
         owned = (slot > 0) & (((slot - 1) >> 2) == me)
         local = jnp.where(owned, ((slot - 1) & 3) + 1, local)
@@ -131,7 +132,8 @@
     low_hot, high_hot = [], []
     for k in range(FOOT):
         rows = slice(P_DEV * k, P_DEV * k + P_DEV)
-        offset = jnp.sum(jnp.where(mine, offset_ref[k : k + 1, :], 0), axis=1, keepdims=True)
+        offset = offset_ref[k : k + 1, :].astype(jnp.float32)
+        offset = jnp.sum(jnp.where(mine, offset, 0.0), axis=1, keepdims=True).astype(jnp.int32)
         block = offset >> 8
         low_hot.append(jnp.where(pick == block * P_DEV + pulse, 1.0, 0.0))
         block = jnp.minimum(block + 1, BLOCKS - 1)
@@ -321,7 +323,7 @@
     bf16, f32, i32 = jnp.bfloat16, jnp.float32, jnp.int32
     shape = jax.ShapeDtypeStruct
     window = pltpu.VMEM((ROWS + P_DEV * (SPANS - 1), 3 * TILE), bf16)
-    tail = lax.ppermute(echoes, "band", [(i, i - 1) for i in range(1, N_BAND)])
+    tail = lax.ppermute(echoes[:, :, :TAPS], "band", [(i, i - 1) for i in range(1, N_BAND)])
     taps = kernel(
         taps_kernel, "taps", shape((TILE, 2 * TILE * SPANS), bf16), cost=8 << 20
     )(replica)

time: 65 us -> 64.8 us (level)
  local copies, waits for them, and re-layouts: 0.86 us -> 1.83 us
    slice x0 -> x1, local copies, waits for them, and re-layouts: none -> 0.97 us  [on_device(): echoes[:, :, :TAPS]]
  transfers between devices with their start and end apart: 2 -> 2, of which waited for: 2 -> 1; matrix products, arithmetic and copies ran while one was open for 0% -> 0% of each run, Pallas kernels for 4% -> 4%
where the time goes in v5:
time: 64.8 us; the launch traced here: 64.5 us
  blocking collectives  47.8 us (74%)
  Pallas kernels  7.71 us (12%)
  starting transfers between devices  5.37 us (8%)
  local copies, waits for them, and re-layouts  1.83 us (3%)
  waiting for transfers between devices  1.02 us (2%)
  between operations  0.73 us (1%)
    all_to_all x1, blocking collectives, on_device(): lax.all_to_all(rows, 'pulse', split_axis=0, concat_axis=0, tiled=True)  26.8 us
    all_to_all x1, blocking collectives, on_device(): lax.all_to_all(spread, ('pulse', 'band'), split_axis=0, concat_axis=0, ax...  21 us
    ppermute x1, starting transfers between devices, on_device(): lax.ppermute(echoes[:, :, :TAPS], 'band', [(i, i - 1) for i in range(1, N...  5.15 us
    pallas_call x1, Pallas kernels, on_device(): kernel(owner_kernel, 'owner', [shape((2, TILES_DEV, TILE, TILE), f32), sh...  3.31 us
    pallas_call x1, Pallas kernels, on_device(): kernel(prep_kernel, 'prep', [shape((2 * TILE, KDIM), bf16), shape((N_PULS...  1.81 us
  transfers between devices with their start and end apart: 2, of which 1 were waited for; matrix products, arithmetic and copies ran while one was open for 0% of the time, Pallas kernels for 4%

profile of v5, /device:TPU:1, one launch (start us, length us, event | category | flops | bytes accessed | tf_op | source)
XLA Modules:
  0.0 64.5 jit_solution(17703689123410885841)
XLA Ops:
  0.6 0.0 copy-start
  0.6 0.0 copy-start.1
  0.6 1.0 %slice.3 = bf16[2,16,2048]{2,1,0:T(8,128)(2,1)S(1)} slice(bf16[2,16,4096]{2,1,0:T(8,128)(2,1)} %echo_ref.1), slice={[0:2], [0:16], [0:2048]} | slice | bytes 262144 | tf_op jit(solution)/shard_map/slice | solution.py:326
  1.6 5.1 %collective-permute-start = (bf16[2,16,2048]{2,1,0:T(8,128)(2,1)S(1)}, bf16[2,16,2048]{2,1,0:T(8,128)(2,1)S(1)}, u32[]{:S(2)}, u32[]{:S(2)}) collective-permute-start(bf16[2,16,2048]{2,1,0:T(8,128)(2,1)S(1)} %slice.3), channel_id=1, source_target_pairs={{1,0},{2,1},{3,2},{4,3},{5,4},{6,5},{7,6},{9,8},{10,9},{11,10},{12... | collective-permute-start | bytes 393224 | tf_op jit(solution)/shard_map/ppermute | solution.py:326
  6.8 0.0 copy-start.2
  6.8 0.7 %copy-done.2 = bf16[2,2048]{1,0:T(2,128)(2,1)S(1)} copy-done((bf16[2,2048]{1,0:T(2,128)(2,1)S(1)}, bf16[2,2048]{1,0:T(2,128)(2,1)}, u32[]{:S(2)}) %copy-start.2) | copy-done | bytes 8216
  7.5 0.0 copy-start.3
  7.5 0.0 copy-start.4
  7.5 0.0 copy-start.5
  7.5 0.5 taps.1.taps_ref
  8.0 0.0 copy-done
  8.0 0.0 copy-done.1
  8.0 0.1 copy-done.3
  8.2 0.0 copy-done.4
  8.2 0.0 copy-done.5
  8.2 1.8 %prep.1 = (bf16[512,1024]{1,0:T(8,128)(2,1)S(1)}, s32[32,128]{1,0:T(8,128)S(1)}, s32[32,128]{1,0:T(8,128)S(1)}, bf16[256,256]{1,0:T(8,128)(2,1)S(1)}, s32[128,12...) custom-call(bf16[256,4608]{1,0:T(8,128)(2,1)S(1)} %taps.1.taps_ref, ...), custom_call_target="tpu_custom_call" | custom-call | bytes 12582912 | tf_op jit(solution)/shard_map/prep/pallas_call | solution.py:330
  10.0 0.0 collective-permute-done.tail_ref
  10.0 1.2 %rows.1 = bf16[32,2,16,256]{3,2,1,0:T(8,128)(2,1)S(1)} custom-call(bf16[2,16,2048]{2,1,0:T(8,128)(2,1)S(1)} %collective-permute-done.tail_ref, bf16[256,4608]{1,0:T(8,128)(2,1)S(1)} %taps.1.taps_ref, f32[2,256,256]{2,1,0:T(8,128)S(1)} %get-tuple-element.12.near_ref, bf16[256,256]{1,0:T(8,128)(2,1)S(1)} %get-tuple-element.13.hot_ref, ...), custom_call_target="tpu_custom_call" | custom-call | tf_op jit(solution)/shard_map/rows/pallas_call | solution.py:345
  11.2 26.8 %all_to_all.10.arrived_ref = bf16[32,2,16,256]{3,2,1,0:T(8,128)(2,1)S(1)} all-to-all(bf16[32,2,16,256]{3,2,1,0:T(8,128)(2,1)S(1)} %rows.1), channel_id=1, replica_groups=mesh['pulse'=32,'band'=8] {'pulse'}, dimensions={0} | all-to-all | bytes 1048576 | tf_op jit(solution)/shard_map/all_to_all | solution.py:351
  38.0 3.3 %owner.1 = (f32[2,4,256,256]{3,2,1,0:T(8,128)}, f32[4,128]{1,0:T(4,128)S(1)}) custom-call(s32[32,128]{1,0:T(8,128)S(1)} %get-tuple-element.11.local_ref, bf16[32,2,16,256]{3,2,1,0:T(8,128)(2,1)S(1)} %all_to_all.10.arrived_ref, bf16[512,1024]{1,0:T(8,128)(2,1)S(1)} %get-tuple-element.17.steer_ref), custom_call_target="tpu_custom_call" | custom-call | tf_op jit(solution)/shard_map/owner/pallas_call | solution.py:352
  41.4 0.2 collective-permute-start.1
  41.6 1.0 %collective-permute-done.1.other_ref = f32[4,128]{1,0:T(4,128)S(1)} collective-permute-done((f32[4,128]{1,0:T(4,128)S(1)}, f32[4,128]{1,0:T(4,128)S(1)}, u32[]{:S(2)}, u32[]{:S(2)}) %collective-permute-start.1) | collective-permute-done | bytes 2080 | tf_op jit(solution)/shard_map/ppermute | solution.py:368
  42.6 21.0 %all_to_all.11.parts_ref = bf16[128,4,128]{2,1,0:T(4,128)(2,1)S(1)} all-to-all(bf16[128,4,128]{2,1,0:T(4,128)(2,1)S(1)} %spread.1), channel_id=1, replica_groups={{0,2,4,6,8,10,12,14,16,18,20,22,24,26,28,30,32,34,36,38,40,42,44,46,48,..., dimensions={0} | all-to-all | bytes 262144 | tf_op jit(solution)/shard_map/all_to_all | solution.py:373
  63.7 0.8 %final.1 = f32[1,16]{1,0:T(1,128)} custom-call(bf16[128,4,128]{2,1,0:T(4,128)(2,1)S(1)} %all_to_all.11.parts_ref), custom_call_target="tpu_custom_call" | custom-call | tf_op jit(solution)/shard_map/final/pallas_call | solution.py:381
  (1 shorter events, 0.0 us)
Async XLA Ops:
  0.6 7.4 %copy-start = (bf16[2,16,4096]{2,1,0:T(8,128)(2,1)S(1)}, bf16[2,16,4096]{2,1,0:T(8,128)(2,1)}, u32[]{:S(2)}) copy-start(bf16[2,16,4096]{2,1,0:T(8,128)(2,1)} %echo_ref.1) | copy-start | bytes 786436
  0.6 7.4 %copy-start.1 = (s32[512,8]{0,1:T(8,128)S(1)}, s32[512,8]{0,1:T(8,128)}, u32[]{:S(2)}) copy-start(s32[512,8]{0,1:T(8,128)} %param.11) | copy-start | bytes 49156
  1.6 8.4 %collective-permute-start = (bf16[2,16,2048]{2,1,0:T(8,128)(2,1)S(1)}, bf16[2,16,2048]{2,1,0:T(8,128)(2,1)S(1)}, u32[]{:S(2)}, u32[]{:S(2)}) collective-permute-start(bf16[2,16,2048]{2,1,0:T(8,128)(2,1)S(1)} %slice.3), channel_id=1, source_target_pairs={{1,0},{2,1},{3,2},{4,3},{5,4},{6,5},{7,6},{9,8},{10,9},{11,10},{12... | collective-permute-start | bytes 393224 | tf_op jit(solution)/shard_map/ppermute | solution.py:326
  6.8 0.7 %copy-start.2 = (bf16[2,2048]{1,0:T(2,128)(2,1)S(1)}, bf16[2,2048]{1,0:T(2,128)(2,1)}, u32[]{:S(2)}) copy-start(bf16[2,2048]{1,0:T(2,128)(2,1)} %replica_ref.1) | copy-start | bytes 24580
  7.5 0.7 %copy-start.3 = (f32[3,512]{1,0:T(4,128)S(1)}, f32[3,512]{1,0:T(4,128)}, u32[]{:S(2)}) copy-start(f32[3,512]{1,0:T(4,128)} %angle_ref.1) | copy-start | bytes 18436
  7.5 0.7 %copy-start.4 = (s32[32,8]{0,1:T(8,128)S(1)}, s32[32,8]{0,1:T(8,128)}, u32[]{:S(2)}) copy-start(s32[32,8]{0,1:T(8,128)} %param.9) | copy-start | bytes 3076
  7.5 0.7 %copy-start.5 = (s32[128]{0:T(128)S(1)}, s32[128]{0:T(128)}, u32[]{:S(2)}) copy-start(s32[128]{0:T(128)} %param.10) | copy-start | bytes 1540
  41.4 1.2 %collective-permute-start.1 = (f32[4,128]{1,0:T(4,128)S(1)}, f32[4,128]{1,0:T(4,128)S(1)}, u32[]{:S(2)}, u32[]{:S(2)}) collective-permute-start(f32[4,128]{1,0:T(4,128)S(1)} %get-tuple-element.19.own_ref), channel_id=1, source_target_pairs={{0,1},{1,0},{2,3},{3,2},{4,5},{5,4},{6,7},{7,6},{8,9},{9,8},{10,11... | collective-permute-start | bytes 6152 | tf_op jit(solution)/shard_map/ppermute | solution.py:368

commit v6 on v5

--- a/solution.py
+++ b/solution.py
@@ -53,12 +53,13 @@
                     taps_ref[row : row + 16, col : col + LANE] = piece
 
 
-def fill_steer(angle_ref, steer_ref):
-    step = lax.broadcasted_iota(jnp.int32, (16, PULSES), 0).astype(jnp.float32)
-    omega = angle_ref[0:1, :]
-    fine, coarse = step * omega, (16.0 * step) * omega
-    fine_cos, fine_sin = jnp.cos(fine), jnp.sin(fine)
-    coarse_cos, coarse_sin = jnp.cos(coarse), jnp.sin(coarse)
+def fill_steer(fine_cos, fine_sin, steer_ref):
+    coarse_cos, coarse_sin = fine_cos, fine_sin
+    for _ in range(4):
+        coarse_cos, coarse_sin = (
+            coarse_cos * coarse_cos - coarse_sin * coarse_sin,
+            2.0 * coarse_cos * coarse_sin,
+        )
     for a in range(TILE // 16):
         ca, sa = coarse_cos[a : a + 1], coarse_sin[a : a + 1]
         cosine = (fine_cos * ca - fine_sin * sa).astype(jnp.bfloat16)
@@ -94,7 +95,6 @@
     listed_ref,
 ):
     me = lax.axis_index("pulse")
-    fill_steer(angle_ref, steer_ref)
 
     for n in range(BLOCKS):
         rows = slice(P_DEV * n, P_DEV * n + P_DEV)
@@ -125,8 +125,13 @@
     tiles = jnp.maximum(listed_ref[pl.ds(me, 1), :], 0).astype(jnp.float32)
     kappa = jnp.sum(jnp.where(mine, angle_ref[1:2, :], 0.0), axis=1, keepdims=True)
     phase = jnp.sum(jnp.where(mine, angle_ref[2:3, :], 0.0), axis=1, keepdims=True)
+    tiles = jnp.concatenate([tiles, jnp.zeros((1, LANE - FOOT), jnp.float32)], axis=1)
     turn = kappa * tiles + phase
-    cosine, sine = jnp.cos(turn), jnp.sin(turn)
+    step = lax.broadcasted_iota(jnp.int32, (P_DEV, PULSES), 0).astype(jnp.float32)
+    angles = jnp.concatenate([step * angle_ref[0:1, :], turn], axis=1)
+    cosine, sine = jnp.cos(angles), jnp.sin(angles)
+    fill_steer(cosine[:, :PULSES], sine[:, :PULSES], steer_ref)
+    cosine, sine = cosine[:, PULSES:], sine[:, PULSES:]
     pulse = lax.broadcasted_iota(jnp.int32, (P_DEV, ROWS), 0)
     pick = lax.broadcasted_iota(jnp.int32, (P_DEV, ROWS), 1)
     low_hot, high_hot = [], []

time: 64.8 us -> 64.8 us (level)
  transfers between devices with their start and end apart: 2 -> 2, of which waited for: 1 -> 1; matrix products, arithmetic and copies ran while one was open for 0% -> 0% of each run, Pallas kernels for 4% -> 3%
where the time goes in v6:
time: 64.8 us; the launch traced here: 64.5 us
  blocking collectives  47.9 us (74%)
  Pallas kernels  7.61 us (12%)
  starting transfers between devices  5.24 us (8%)
  local copies, waits for them, and re-layouts  1.83 us (3%)
  waiting for transfers between devices  1.15 us (2%)
  between operations  0.74 us (1%)
    all_to_all x1, blocking collectives, on_device(): lax.all_to_all(rows, 'pulse', split_axis=0, concat_axis=0, tiled=True)  27.1 us
    all_to_all x1, blocking collectives, on_device(): lax.all_to_all(spread, ('pulse', 'band'), split_axis=0, concat_axis=0, ax...  20.9 us
    ppermute x1, starting transfers between devices, on_device(): lax.ppermute(echoes[:, :, :TAPS], 'band', [(i, i - 1) for i in range(1, N...  5.15 us
    pallas_call x1, Pallas kernels, on_device(): kernel(owner_kernel, 'owner', [shape((2, TILES_DEV, TILE, TILE), f32), sh...  3.31 us
    pallas_call x1, Pallas kernels, on_device(): kernel(prep_kernel, 'prep', [shape((2 * TILE, KDIM), bf16), shape((N_PULS...  1.71 us
  transfers between devices with their start and end apart: 2, of which 1 were waited for; matrix products, arithmetic and copies ran while one was open for 0% of the time, Pallas kernels for 3%

profile of v6, /device:TPU:1, one launch (start us, length us, event | category | flops | bytes accessed | tf_op | source)
XLA Modules:
  0.0 64.5 jit_solution(14827938599060306569)
XLA Ops:
  0.6 0.0 copy-start
  0.6 0.0 copy-start.1
  0.6 1.0 %slice.3 = bf16[2,16,2048]{2,1,0:T(8,128)(2,1)S(1)} slice(bf16[2,16,4096]{2,1,0:T(8,128)(2,1)} %echo_ref.1), slice={[0:2], [0:16], [0:2048]} | slice | bytes 262144 | tf_op jit(solution)/shard_map/slice | solution.py:331
  1.6 5.1 %collective-permute-start = (bf16[2,16,2048]{2,1,0:T(8,128)(2,1)S(1)}, bf16[2,16,2048]{2,1,0:T(8,128)(2,1)S(1)}, u32[]{:S(2)}, u32[]{:S(2)}) collective-permute-start(bf16[2,16,2048]{2,1,0:T(8,128)(2,1)S(1)} %slice.3), channel_id=1, source_target_pairs={{1,0},{2,1},{3,2},{4,3},{5,4},{6,5},{7,6},{9,8},{10,9},{11,10},{12... | collective-permute-start | bytes 393224 | tf_op jit(solution)/shard_map/ppermute | solution.py:331
  6.8 0.0 copy-start.2
  6.8 0.7 %copy-done.2 = bf16[2,2048]{1,0:T(2,128)(2,1)S(1)} copy-done((bf16[2,2048]{1,0:T(2,128)(2,1)S(1)}, bf16[2,2048]{1,0:T(2,128)(2,1)}, u32[]{:S(2)}) %copy-start.2) | copy-done | bytes 8216
  7.5 0.0 copy-start.3
  7.5 0.0 copy-start.4
  7.5 0.0 copy-start.5
  7.5 0.5 taps.1.taps_ref
  8.0 0.0 copy-done
  8.0 0.0 copy-done.1
  8.0 0.1 copy-done.3
  8.2 0.0 copy-done.4
  8.2 0.0 copy-done.5
  8.2 1.7 %prep.1 = (bf16[512,1024]{1,0:T(8,128)(2,1)S(1)}, s32[32,128]{1,0:T(8,128)S(1)}, s32[32,128]{1,0:T(8,128)S(1)}, bf16[256,256]{1,0:T(8,128)(2,1)S(1)}, s32[128,12...) custom-call(bf16[256,4608]{1,0:T(8,128)(2,1)S(1)} %taps.1.taps_ref, ...), custom_call_target="tpu_custom_call" | custom-call | bytes 12582912 | tf_op jit(solution)/shard_map/prep/pallas_call | solution.py:335
  9.9 0.0 collective-permute-done.tail_ref
  9.9 1.2 %rows.1 = bf16[32,2,16,256]{3,2,1,0:T(8,128)(2,1)S(1)} custom-call(bf16[2,16,2048]{2,1,0:T(8,128)(2,1)S(1)} %collective-permute-done.tail_ref, bf16[256,4608]{1,0:T(8,128)(2,1)S(1)} %taps.1.taps_ref, f32[2,256,256]{2,1,0:T(8,128)S(1)} %get-tuple-element.12.near_ref, bf16[256,256]{1,0:T(8,128)(2,1)S(1)} %get-tuple-element.13.hot_ref, ...), custom_call_target="tpu_custom_call" | custom-call | tf_op jit(solution)/shard_map/rows/pallas_call | solution.py:350
  11.1 27.1 %all_to_all.10.arrived_ref = bf16[32,2,16,256]{3,2,1,0:T(8,128)(2,1)S(1)} all-to-all(bf16[32,2,16,256]{3,2,1,0:T(8,128)(2,1)S(1)} %rows.1), channel_id=1, replica_groups=mesh['pulse'=32,'band'=8] {'pulse'}, dimensions={0} | all-to-all | bytes 1048576 | tf_op jit(solution)/shard_map/all_to_all | solution.py:356
  38.2 3.3 %owner.1 = (f32[2,4,256,256]{3,2,1,0:T(8,128)}, f32[4,128]{1,0:T(4,128)S(1)}) custom-call(s32[32,128]{1,0:T(8,128)S(1)} %get-tuple-element.11.local_ref, bf16[32,2,16,256]{3,2,1,0:T(8,128)(2,1)S(1)} %all_to_all.10.arrived_ref, bf16[512,1024]{1,0:T(8,128)(2,1)S(1)} %get-tuple-element.17.steer_ref), custom_call_target="tpu_custom_call" | custom-call | tf_op jit(solution)/shard_map/owner/pallas_call | solution.py:357
  41.5 0.1 collective-permute-start.1
  41.6 1.1 %collective-permute-done.1.other_ref = f32[4,128]{1,0:T(4,128)S(1)} collective-permute-done((f32[4,128]{1,0:T(4,128)S(1)}, f32[4,128]{1,0:T(4,128)S(1)}, u32[]{:S(2)}, u32[]{:S(2)}) %collective-permute-start.1) | collective-permute-done | bytes 2080 | tf_op jit(solution)/shard_map/ppermute | solution.py:373
  42.8 20.9 %all_to_all.11.parts_ref = bf16[128,4,128]{2,1,0:T(4,128)(2,1)S(1)} all-to-all(bf16[128,4,128]{2,1,0:T(4,128)(2,1)S(1)} %spread.1), channel_id=1, replica_groups={{0,2,4,6,8,10,12,14,16,18,20,22,24,26,28,30,32,34,36,38,40,42,44,46,48,..., dimensions={0} | all-to-all | bytes 262144 | tf_op jit(solution)/shard_map/all_to_all | solution.py:378
  63.7 0.8 %final.1 = f32[1,16]{1,0:T(1,128)} custom-call(bf16[128,4,128]{2,1,0:T(4,128)(2,1)S(1)} %all_to_all.11.parts_ref), custom_call_target="tpu_custom_call" | custom-call | tf_op jit(solution)/shard_map/final/pallas_call | solution.py:386
  (1 shorter events, 0.0 us)
Async XLA Ops:
  0.6 7.4 %copy-start = (bf16[2,16,4096]{2,1,0:T(8,128)(2,1)S(1)}, bf16[2,16,4096]{2,1,0:T(8,128)(2,1)}, u32[]{:S(2)}) copy-start(bf16[2,16,4096]{2,1,0:T(8,128)(2,1)} %echo_ref.1) | copy-start | bytes 786436
  0.6 7.4 %copy-start.1 = (s32[512,8]{0,1:T(8,128)S(1)}, s32[512,8]{0,1:T(8,128)}, u32[]{:S(2)}) copy-start(s32[512,8]{0,1:T(8,128)} %param.11) | copy-start | bytes 49156
  1.6 8.3 %collective-permute-start = (bf16[2,16,2048]{2,1,0:T(8,128)(2,1)S(1)}, bf16[2,16,2048]{2,1,0:T(8,128)(2,1)S(1)}, u32[]{:S(2)}, u32[]{:S(2)}) collective-permute-start(bf16[2,16,2048]{2,1,0:T(8,128)(2,1)S(1)} %slice.3), channel_id=1, source_target_pairs={{1,0},{2,1},{3,2},{4,3},{5,4},{6,5},{7,6},{9,8},{10,9},{11,10},{12... | collective-permute-start | bytes 393224 | tf_op jit(solution)/shard_map/ppermute | solution.py:331
  6.8 0.7 %copy-start.2 = (bf16[2,2048]{1,0:T(2,128)(2,1)S(1)}, bf16[2,2048]{1,0:T(2,128)(2,1)}, u32[]{:S(2)}) copy-start(bf16[2,2048]{1,0:T(2,128)(2,1)} %replica_ref.1) | copy-start | bytes 24580
  7.5 0.7 %copy-start.3 = (f32[3,512]{1,0:T(4,128)S(1)}, f32[3,512]{1,0:T(4,128)}, u32[]{:S(2)}) copy-start(f32[3,512]{1,0:T(4,128)} %angle_ref.1) | copy-start | bytes 18436
  7.5 0.7 %copy-start.4 = (s32[32,8]{0,1:T(8,128)S(1)}, s32[32,8]{0,1:T(8,128)}, u32[]{:S(2)}) copy-start(s32[32,8]{0,1:T(8,128)} %param.9) | copy-start | bytes 3076
  7.5 0.7 %copy-start.5 = (s32[128]{0:T(128)S(1)}, s32[128]{0:T(128)}, u32[]{:S(2)}) copy-start(s32[128]{0:T(128)} %param.10) | copy-start | bytes 1540
  41.5 1.2 %collective-permute-start.1 = (f32[4,128]{1,0:T(4,128)S(1)}, f32[4,128]{1,0:T(4,128)S(1)}, u32[]{:S(2)}, u32[]{:S(2)}) collective-permute-start(f32[4,128]{1,0:T(4,128)S(1)} %get-tuple-element.19.own_ref), channel_id=1, source_target_pairs={{0,1},{1,0},{2,3},{3,2},{4,5},{5,4},{6,7},{7,6},{8,9},{9,8},{10,11... | collective-permute-start | bytes 6152 | tf_op jit(solution)/shard_map/ppermute | solution.py:373

commit v7 on v5

--- a/solution.py
+++ b/solution.py
@@ -234,13 +234,10 @@
     local_ref,
     arrived_ref,
     steer_ref,
-    image_hbm,
+    flat_ref,
     grad_ref,
     rows_ref,
     weight_ref,
-    flat_ref,
-    image_ref,
-    image_sem,
 ):
     for d in range(N_PULSE):
         slot = local_ref[d, 0]
@@ -251,24 +248,13 @@
                 rows_ref[row : row + P_DEV, TILE * l : TILE * l + TILE] = jnp.where(
                     slot == l + 1, piece, jnp.zeros_like(piece)
                 )
-    copies, sums = [], []
-
-    def write_out(l):
-        cols = slice(TILE * l, TILE * l + TILE)
-        for c in range(2):
-            image_ref[l, c] = flat_ref[TILE * c : TILE * c + TILE, cols].T
-            copy = pltpu.make_async_copy(image_ref.at[l, c], image_hbm.at[c, l], image_sem.at[l, c])
-            copy.start()
-            copies.append(copy)
-
+    sums = []
     for l in range(TILES_DEV):
         cols = slice(TILE * l, TILE * l + TILE)
         total = lax.dot_general(
             steer_ref[...], rows_ref[:, cols], NN, preferred_element_type=jnp.float32
         )
         flat_ref[:, cols] = total
-        if l > 0:
-            write_out(l - 1)
         real, imag = total[:TILE], total[TILE:]
         power = real * real + imag * imag
         weight_ref[:TILE, cols] = (-power * imag).astype(jnp.bfloat16)
@@ -278,16 +264,17 @@
         back = lax.dot_general(
             weight_ref[...], rows_ref[cols, :], NT, preferred_element_type=jnp.float32
         )
-        if h == 0:
-            write_out(TILES_DEV - 1)
         sums.append(
             jnp.sum(back * steer_ref[:, cols].astype(jnp.float32), axis=0, keepdims=True)
         )
     halves = [-4.0 * (sums[h] + sums[h + 2]) for h in range(2)]
     for c in range(PULSES // LANE):
         grad_ref[c : c + 1, :] = halves[c // 2][:, LANE * (c % 2) : LANE * (c % 2) + LANE]
-    for copy in copies:
-        copy.wait()
+
+
+def image_kernel(flat_ref, spread_ref, out_ref):
+    for comp in range(2):
+        out_ref[comp, 0] = flat_ref[TILE * comp : TILE * comp + TILE, :].T
 
 
 def spread_kernel(own_ref, other_ref, out_ref):
@@ -349,20 +336,16 @@
         scratch=[window, pltpu.VMEM((2, (SPANS - 1) * P_DEV, TILE), f32)],
     )(tail, taps, near, hot, shift, turn, slots)
     arrived = lax.all_to_all(rows, "pulse", split_axis=0, concat_axis=0, tiled=True)
-    image, grad = kernel(
+    flat, grad = kernel(
         owner_kernel,
         "owner",
         [
-            shape((2, TILES_DEV, TILE, TILE), f32),
+            shape((2 * TILE, TILES_DEV * TILE), f32),
             shape((PULSES // LANE, LANE), f32),
         ],
-        out_specs=[pl.BlockSpec(memory_space=pl.ANY), pl.BlockSpec(memory_space=pltpu.VMEM)],
         scratch=[
             pltpu.VMEM((KDIM, TILES_DEV * TILE), bf16),
             pltpu.VMEM((2 * TILE, TILES_DEV * TILE), bf16),
-            pltpu.VMEM((2 * TILE, TILES_DEV * TILE), f32),
-            pltpu.VMEM((TILES_DEV, 2, TILE, TILE), f32),
-            pltpu.SemaphoreType.DMA((TILES_DEV, 2)),
         ],
     )(local, arrived, steer)
     other = lax.ppermute(grad, "band", [(i, i ^ 1) for i in range(N_BAND)])
@@ -370,6 +353,17 @@
     spread = kernel(spread_kernel, "spread", shape((chips, PULSES // LANE, LANE), bf16))(
         grad, other
     )
+    image = kernel(
+        image_kernel,
+        "image",
+        shape((2, TILES_DEV, TILE, TILE), f32),
+        grid=(TILES_DEV,),
+        in_specs=[
+            pl.BlockSpec((2 * TILE, TILE), lambda l: (0, l)),
+            pl.BlockSpec(memory_space=pl.ANY),
+        ],
+        out_specs=pl.BlockSpec((2, 1, TILE, TILE), lambda l: (0, l, 0, 0)),
+    )(flat, spread)
     parts = lax.all_to_all(
         spread,
         ("pulse", "band"),

time: 64.8 us -> 64.7 us (level)
  blocking collectives: 47.8 us -> 26.8 us
  starting transfers between devices: 5.37 us -> 15.3 us
  waiting for transfers between devices: 1.02 us -> 9.8 us
  Pallas kernels: 7.71 us -> 9.89 us
    all_to_all x1 -> x0, blocking collectives: 21 us -> none  [on_device(): lax.all_to_all(spread, ('pulse', 'band'), split_axis=0, concat_axis=0, ax...]
    all_to_all x0 -> x1, starting transfers between devices: none -> 9.97 us  [on_device(): lax.all_to_all(spread, ('pulse', 'band'), split_axis=0, concat_axis=0, ax...]
    all_to_all x0 -> x1, waiting for transfers between devices: none -> 8.77 us  [on_device(): lax.all_to_all(spread, ('pulse', 'band'), split_axis=0, concat_axis=0, ax...]
    pallas_call x1 -> x2, Pallas kernels: 3.31 us -> 4.87 us  [the longest x1 2.52 us: on_device(): kernel(owner_kernel, 'owner', [shape((2 * TILE, TILES_DEV * TILE), f32),...]
  transfers between devices with their start and end apart: 2 -> 3, of which waited for: 1 -> 2; matrix products, arithmetic and copies ran while one was open for 0% -> 0% of each run, Pallas kernels for 4% -> 7%
where the time goes in v7:
time: 64.7 us; the launch traced here: 64.4 us
  blocking collectives  26.8 us (41%)
  starting transfers between devices  15.3 us (24%)
  Pallas kernels  9.89 us (15%)
  waiting for transfers between devices  9.8 us (15%)
  local copies, waits for them, and re-layouts  1.83 us (3%)
  between operations  0.73 us (1%)
    all_to_all x1, blocking collectives, on_device(): lax.all_to_all(rows, 'pulse', split_axis=0, concat_axis=0, tiled=True)  26.8 us
    all_to_all x1, starting transfers between devices, on_device(): lax.all_to_all(spread, ('pulse', 'band'), split_axis=0, concat_axis=0, ax...  9.97 us
    all_to_all x1, waiting for transfers between devices, on_device(): lax.all_to_all(spread, ('pulse', 'band'), split_axis=0, concat_axis=0, ax...  8.77 us
    ppermute x1, starting transfers between devices, on_device(): lax.ppermute(echoes[:, :, :TAPS], 'band', [(i, i - 1) for i in range(1, N...  5.15 us
    pallas_call x1, Pallas kernels, on_device(): kernel(owner_kernel, 'owner', [shape((2 * TILE, TILES_DEV * TILE), f32),...  2.52 us
    pallas_call x1, Pallas kernels, on_device(): kernel(image_kernel, 'image', shape((2, TILES_DEV, TILE, TILE), f32), gri...  2.34 us
    pallas_call x1, Pallas kernels, on_device(): kernel(prep_kernel, 'prep', [shape((2 * TILE, KDIM), bf16), shape((N_PULS...  1.81 us
  transfers between devices with their start and end apart: 3, of which 2 were waited for; matrix products, arithmetic and copies ran while one was open for 0% of the time, Pallas kernels for 7%

profile of v7, /device:TPU:1, one launch (start us, length us, event | category | flops | bytes accessed | tf_op | source)
XLA Modules:
  0.0 64.4 jit_solution(8270326852498043808)
XLA Ops:
  0.6 0.0 copy-start
  0.6 0.0 copy-start.1
  0.6 1.0 %slice.3 = bf16[2,16,2048]{2,1,0:T(8,128)(2,1)S(1)} slice(bf16[2,16,4096]{2,1,0:T(8,128)(2,1)} %echo_ref.1), slice={[0:2], [0:16], [0:2048]} | slice | bytes 262144 | tf_op jit(solution)/shard_map/slice | solution.py:313
  1.6 5.1 %collective-permute-start = (bf16[2,16,2048]{2,1,0:T(8,128)(2,1)S(1)}, bf16[2,16,2048]{2,1,0:T(8,128)(2,1)S(1)}, u32[]{:S(2)}, u32[]{:S(2)}) collective-permute-start(bf16[2,16,2048]{2,1,0:T(8,128)(2,1)S(1)} %slice.3), channel_id=1, source_target_pairs={{1,0},{2,1},{3,2},{4,3},{5,4},{6,5},{7,6},{9,8},{10,9},{11,10},{12... | collective-permute-start | bytes 393224 | tf_op jit(solution)/shard_map/ppermute | solution.py:313
  6.8 0.0 copy-start.2
  6.8 0.7 %copy-done.2 = bf16[2,2048]{1,0:T(2,128)(2,1)S(1)} copy-done((bf16[2,2048]{1,0:T(2,128)(2,1)S(1)}, bf16[2,2048]{1,0:T(2,128)(2,1)}, u32[]{:S(2)}) %copy-start.2) | copy-done | bytes 8216
  7.5 0.0 copy-start.3
  7.5 0.0 copy-start.4
  7.5 0.0 copy-start.5
  7.5 0.5 taps.1.taps_ref
  8.0 0.0 copy-done
  8.0 0.0 copy-done.1
  8.0 0.1 copy-done.3
  8.2 0.0 copy-done.4
  8.2 0.0 copy-done.5
  8.2 1.8 %prep.1 = (bf16[512,1024]{1,0:T(8,128)(2,1)S(1)}, s32[32,128]{1,0:T(8,128)S(1)}, s32[32,128]{1,0:T(8,128)S(1)}, bf16[256,256]{1,0:T(8,128)(2,1)S(1)}, s32[128,12...) custom-call(bf16[256,4608]{1,0:T(8,128)(2,1)S(1)} %taps.1.taps_ref, ...), custom_call_target="tpu_custom_call" | custom-call | bytes 12582912 | tf_op jit(solution)/shard_map/prep/pallas_call | solution.py:317
  10.0 0.0 collective-permute-done.tail_ref
  10.0 1.2 %rows.1 = bf16[32,2,16,256]{3,2,1,0:T(8,128)(2,1)S(1)} custom-call(bf16[2,16,2048]{2,1,0:T(8,128)(2,1)S(1)} %collective-permute-done.tail_ref, bf16[256,4608]{1,0:T(8,128)(2,1)S(1)} %taps.1.taps_ref, f32[2,256,256]{2,1,0:T(8,128)S(1)} %get-tuple-element.12.near_ref, bf16[256,256]{1,0:T(8,128)(2,1)S(1)} %get-tuple-element.13.hot_ref, ...), custom_call_target="tpu_custom_call" | custom-call | tf_op jit(solution)/shard_map/rows/pallas_call | solution.py:332
  11.2 26.8 %all_to_all.10.arrived_ref = bf16[32,2,16,256]{3,2,1,0:T(8,128)(2,1)S(1)} all-to-all(bf16[32,2,16,256]{3,2,1,0:T(8,128)(2,1)S(1)} %rows.1), channel_id=1, replica_groups=mesh['pulse'=32,'band'=8] {'pulse'}, dimensions={0} | all-to-all | bytes 1048576 | tf_op jit(solution)/shard_map/all_to_all | solution.py:338
  38.0 2.5 %owner.1 = (f32[512,1024]{1,0:T(8,128)S(1)}, f32[4,128]{1,0:T(4,128)S(1)}) custom-call(s32[32,128]{1,0:T(8,128)S(1)} %get-tuple-element.11.local_ref, bf16[32,2,16,256]{3,2,1,0:T(8,128)(2,1)S(1)} %all_to_all.10.arrived_ref, bf16[512,1024]{1,0:T(8,128)(2,1)S(1)} %get-tuple-element.17.steer_ref), custom_call_target="tpu_custom_call" | custom-call | tf_op jit(solution)/shard_map/owner/pallas_call | solution.py:339
  40.6 0.2 collective-permute-start.1
  40.8 1.0 %collective-permute-done.1.other_ref = f32[4,128]{1,0:T(4,128)S(1)} collective-permute-done((f32[4,128]{1,0:T(4,128)S(1)}, f32[4,128]{1,0:T(4,128)S(1)}, u32[]{:S(2)}, u32[]{:S(2)}) %collective-permute-start.1) | collective-permute-done | bytes 2080 | tf_op jit(solution)/shard_map/ppermute | solution.py:351
  41.8 0.7 %spread.1.spread_ref = bf16[128,4,128]{2,1,0:T(4,128)(2,1)} custom-call(f32[4,128]{1,0:T(4,128)S(1)} %get-tuple-element.19.own_ref, f32[4,128]{1,0:T(4,128)S(1)} %collective-permute-done.1.other_ref), custom_call_target="tpu_custom_call" | custom-call | tf_op jit(solution)/shard_map/spread/pallas_call | solution.py:353
  42.5 10.0 %all-to-all-start.1 = ((bf16[128,4,128]{2,1,0:T(4,128)(2,1)}), bf16[128,4,128]{2,1,0:T(4,128)(2,1)S(1)}, u32[]{:S(2)}, u32[]{:S(2)}) async-start(bf16[128,4,128]{2,1,0:T(4,128)(2,1)} %spread.1.spread_ref), calls=%async_computation.1 | async-start | bytes 262144 | tf_op jit(solution)/shard_map/all_to_all | solution.py:367
  52.5 2.3 %image.1 = f32[2,4,256,256]{3,2,1,0:T(8,128)} custom-call(f32[512,1024]{1,0:T(8,128)S(1)} %get-tuple-element.18.flat_ref, bf16[128,4,128]{2,1,0:T(4,128)(2,1)} %spread.1.spread_ref), custom_call_target="tpu_custom_call" | custom-call | tf_op jit(solution)/shard_map/image/pallas_call | solution.py:356
  54.8 8.8 %all-to-all-done.1.parts_ref = bf16[128,4,128]{2,1,0:T(4,128)(2,1)S(1)} async-done(((bf16[128,4,128]{2,1,0:T(4,128)(2,1)}), bf16[128,4,128]{2,1,0:T(4,128)(2,1)S(1)}, u32[]{:S(2)}, u32[]{:S(2)}) %all-to-all-start.1) | async-done | bytes 131104 | tf_op jit(solution)/shard_map/all_to_all | solution.py:367
  63.6 0.8 %final.1 = f32[1,16]{1,0:T(1,128)} custom-call(bf16[128,4,128]{2,1,0:T(4,128)(2,1)S(1)} %all-to-all-done.1.parts_ref), custom_call_target="tpu_custom_call" | custom-call | tf_op jit(solution)/shard_map/final/pallas_call | solution.py:375
Async XLA Ops:
  0.6 7.4 %copy-start = (bf16[2,16,4096]{2,1,0:T(8,128)(2,1)S(1)}, bf16[2,16,4096]{2,1,0:T(8,128)(2,1)}, u32[]{:S(2)}) copy-start(bf16[2,16,4096]{2,1,0:T(8,128)(2,1)} %echo_ref.1) | copy-start | bytes 786436
  0.6 7.4 %copy-start.1 = (s32[512,8]{0,1:T(8,128)S(1)}, s32[512,8]{0,1:T(8,128)}, u32[]{:S(2)}) copy-start(s32[512,8]{0,1:T(8,128)} %param.11) | copy-start | bytes 49156
  1.6 8.4 %collective-permute-start = (bf16[2,16,2048]{2,1,0:T(8,128)(2,1)S(1)}, bf16[2,16,2048]{2,1,0:T(8,128)(2,1)S(1)}, u32[]{:S(2)}, u32[]{:S(2)}) collective-permute-start(bf16[2,16,2048]{2,1,0:T(8,128)(2,1)S(1)} %slice.3), channel_id=1, source_target_pairs={{1,0},{2,1},{3,2},{4,3},{5,4},{6,5},{7,6},{9,8},{10,9},{11,10},{12... | collective-permute-start | bytes 393224 | tf_op jit(solution)/shard_map/ppermute | solution.py:313
  6.8 0.7 %copy-start.2 = (bf16[2,2048]{1,0:T(2,128)(2,1)S(1)}, bf16[2,2048]{1,0:T(2,128)(2,1)}, u32[]{:S(2)}) copy-start(bf16[2,2048]{1,0:T(2,128)(2,1)} %replica_ref.1) | copy-start | bytes 24580
  7.5 0.7 %copy-start.3 = (f32[3,512]{1,0:T(4,128)S(1)}, f32[3,512]{1,0:T(4,128)}, u32[]{:S(2)}) copy-start(f32[3,512]{1,0:T(4,128)} %angle_ref.1) | copy-start | bytes 18436
  7.5 0.7 %copy-start.4 = (s32[32,8]{0,1:T(8,128)S(1)}, s32[32,8]{0,1:T(8,128)}, u32[]{:S(2)}) copy-start(s32[32,8]{0,1:T(8,128)} %param.9) | copy-start | bytes 3076
  7.5 0.7 %copy-start.5 = (s32[128]{0:T(128)S(1)}, s32[128]{0:T(128)}, u32[]{:S(2)}) copy-start(s32[128]{0:T(128)} %param.10) | copy-start | bytes 1540
  40.6 1.2 %collective-permute-start.1 = (f32[4,128]{1,0:T(4,128)S(1)}, f32[4,128]{1,0:T(4,128)S(1)}, u32[]{:S(2)}, u32[]{:S(2)}) collective-permute-start(f32[4,128]{1,0:T(4,128)S(1)} %get-tuple-element.19.own_ref), channel_id=1, source_target_pairs={{0,1},{1,0},{2,3},{3,2},{4,5},{5,4},{6,7},{7,6},{8,9},{9,8},{10,11... | collective-permute-start | bytes 6152 | tf_op jit(solution)/shard_map/ppermute | solution.py:351
  42.5 21.1 %all-to-all-start.1 = ((bf16[128,4,128]{2,1,0:T(4,128)(2,1)}), bf16[128,4,128]{2,1,0:T(4,128)(2,1)S(1)}, u32[]{:S(2)}, u32[]{:S(2)}) async-start(bf16[128,4,128]{2,1,0:T(4,128)(2,1)} %spread.1.spread_ref), calls=%async_computation.1 | async-start | bytes 262144 | tf_op jit(solution)/shard_map/all_to_all | solution.py:367
